TPU v7x, 128 devices: a whole 4x4x4 slice. The times are simulated.
128 devices in a mesh: mod: 16 (over z, y_hi, core), ex: 8 (over y_lo, x).
Axes of the slice: x: 4, y: 4 (y_hi: 2, y_lo: 2; y = y_hi * 2 + y_lo), z: 4, core: 2. Of those that a mesh axis runs over, the one named last changes fastest.
Arguments:
- queries: bfloat16 [512, 16, 4096], P(('mod', 'ex')), may hold values from -6 to 6
- hessian_inv: bfloat16 [16, 4096, 4096], P('mod', 'ex'), may hold values from -1 to 5
- train_sketch: bfloat16 [16384, 16, 4096], P('ex', 'mod'), may hold values from -0.0234375 to 0.0234375
- module_slot: int32 [16], replicated, may hold values from 0 to 15, each once
- arrival_of: int32 [512], replicated, may hold values from 0 to 511, each once
Outputs:
- scores: float32 [512, 16384], P('mod', 'ex')
Inputs may be any that keep to these rules, and one draw needn't show every extreme that they name: Slot k holds module module_slot[k]; every module is held once. Query k stands in row arrival_of[k] of queries; every row holds one query.
All inputs are finite; a program needn't handle non-finite values.
Results may differ from a plain program's by a relative error of at most 0.0029.
Values may be sent and summed in bfloat16 or wider, within the bound.
No kernel may reach another device: no remote copies, remote signals or barrier semaphores. Data moves between devices by JAX's collectives and lax.ppermute only.
A program may use at most 256 MiB of HBM per device.

v0:
```python
import jax
import jax.numpy as jnp
from jax import lax
from jax.sharding import PartitionSpec as P


def precondition(block, hessian_inv):
    return jnp.einsum(
        "qmb,mab->qma", block, hessian_inv, preferred_element_type=jnp.float32
    ).astype(jnp.bfloat16)


def local(queries, hessian_inv, train_sketch, module_slot, arrival_of):
    slotted = jnp.take(queries, module_slot, axis=1)
    widened = lax.all_gather(slotted, "ex", axis=0, tiled=True)
    owned = lax.all_to_all(widened, "mod", split_axis=1, concat_axis=0, tiled=True)
    precond = precondition(owned, hessian_inv)
    ordered = jnp.take(precond, arrival_of, axis=0)
    added = lax.dot_general(
        lax.all_gather(ordered, "ex", axis=2, tiled=True),
        train_sketch,
        (((1, 2), (1, 2)), ((), ())),
        preferred_element_type=jnp.float32,
    )
    result = lax.psum_scatter(added, "mod", scatter_dimension=0, tiled=True)
    return result


def solution(mesh):
    in_specs = (P(("mod", "ex"), None, None), P("mod", "ex", None), P("ex", "mod", None), P(), P())
    out_specs = P("mod", "ex")
    return jax.shard_map(local, mesh=mesh, in_specs=in_specs, out_specs=out_specs, check_vma=False)
```

profile of v0, /device:TPU:1, one launch (start us, length us, event | category | flops | bytes accessed | tf_op | source)
XLA Modules:
  0.0 288.7 jit_solution(8372445556889258293)
XLA Ops:
  6.5 0.0 copy-start
  6.5 0.0 all-gather.3.cloned.1.call-start
  6.5 0.7 compare_select_fusion.1
  7.3 0.7 compare_and_fusion
  7.9 0.0 copy-done
  7.9 2.1 gather_fusion
  10.0 0.9 select_bitcast_fusion
  10.9 0.0 all-gather.3.cloned.1.call-update
  10.9 55.9 %all-gather.3.cloned.1.call-done = bf16[32,16,4096]{2,1,0:T(8,128)(2,1)} async-done(((bf16[4,16,4096]{2,1,0:T(8,128)(2,1)}), bf16[32,16,4096]{2,1,0:T(8,128)(2,1)}) %all-gather.3.cloned.1.call-update) | async-done | bytes 4194320 | tf_op jit(solution)/shard_map/all_gather | solution.py:15
  66.9 6.5 %copy.7 = bf16[32,16,4096]{2,0,1:T(8,128)(2,1)} copy(bf16[32,16,4096]{2,1,0:T(8,128)(2,1)} %all-gather.3.cloned.1.call-done) | data formatting | bytes 8388608 | tf_op jit(solution)/shard_map/all_gather | solution.py:15
  73.3 0.0 copy-start.1
  73.3 7.4 %all-to-all-start = ((bf16[32,16,4096]{2,0,1:T(8,128)(2,1)}), bf16[32,16,4096]{2,0,1:T(8,128)(2,1)}, u32[]{:S(2)}, u32[]{:S(2)}) async-start(bf16[32,16,4096]{2,0,1:T(8,128)(2,1)} %copy.7), calls=%async_computation | async-start | bytes 8388608 | tf_op jit(solution)/shard_map/all_to_all | solution.py:16
  80.7 0.0 all-gather.5.cloned.1.call-start
  80.8 0.0 copy-done.1
  80.8 51.0 %all-to-all-done = bf16[32,16,4096]{2,0,1:T(8,128)(2,1)} async-done(((bf16[32,16,4096]{2,0,1:T(8,128)(2,1)}), bf16[32,16,4096]{2,0,1:T(8,128)(2,1)}, u32[]{:S(2)}, u32[]{:S(2)}) %all-to-all-start) | async-done | bytes 4194336 | tf_op jit(solution)/shard_map/all_to_all | solution.py:16
  131.8 5.8 %fusion.5 = bf16[512,512]{1,0:T(8,128)(2,1)S(1)} fusion(bf16[512,4096]{1,0:T(8,128)(2,1)} %bitcast.3, bf16[1,512,4096]{2,1,0:T(8,128)(2,1)} %param.6), kind=kOutput, calls=%fused_computation.7 | convolution fusion | flops 2147745792 | bytes 8912896 | tf_op jit(solution)/shard_map/qmb,mab->qma/dot_general | solution.py:8
  137.6 2.0 gather_fusion.1
  139.6 0.9 bitcast_select_fusion
  140.6 0.0 all-gather.5.cloned.1.call-update
  140.6 0.0 reduce-scatter.2.cloned.1.call-start
  140.6 48.2 %all-gather.5.cloned.1.call-done = bf16[512,1,4096]{2,0,1:T(8,128)(2,1)} async-done(((bf16[512,1,512]{2,0,1:T(8,128)(2,1)}), bf16[512,1,4096]{2,0,1:T(8,128)(2,1)}) %all-gather.5.cloned.1.call-update) | async-done | bytes 4194320 | tf_op jit(solution)/shard_map/all_gather | solution.py:20
  188.8 15.1 %fusion = f32[512,2048]{1,0:T(8,128)} fusion(bf16[2048,1,4096]{2,0,1:T(8,128)(2,1)} %param.7, bf16[512,1,4096]{2,0,1:T(8,128)(2,1)} %all-gather.5.cloned.1.call-done), kind=kOutput, calls=%fused_computation.2 | convolution fusion | flops 8589934592 | bytes 25165824 | tf_op jit(solution)/shard_map/dot_general | solution.py:19
  203.9 0.0 reduce-scatter.2.cloned.1.call-update
  204.0 78.2 %reduce-scatter.2.cloned.1.call-done = f32[32,2048]{1,0:T(8,128)} async-done(((f32[512,2048]{1,0:T(8,128)}), f32[32,2048]{1,0:T(8,128)}) %reduce-scatter.2.cloned.1.call-update) | async-done | bytes 262160 | tf_op jit(solution)/shard_map/reduce_scatter | solution.py:25
  (4 shorter events, 0.0 us)
Async XLA Ops:
  6.5 1.4 copy-start
  6.5 60.3 %all-gather.3.cloned.1.call-start = ((), (), s32[]{:S(2)}) async-start(), calls=%async_computation.2 | async-start | bytes 4718592 | tf_op jit(solution)/shard_map/all_gather | solution.py:15
  73.3 7.5 %copy-start.1 = (s32[512]{0:T(512)S(1)}, s32[512]{0:T(512)}, u32[]{:S(2)}) copy-start(s32[512]{0:T(512)} %param.9) | copy-start | bytes 6148
  73.3 58.5 %all-to-all-start = ((bf16[32,16,4096]{2,0,1:T(8,128)(2,1)}), bf16[32,16,4096]{2,0,1:T(8,128)(2,1)}, u32[]{:S(2)}, u32[]{:S(2)}) async-start(bf16[32,16,4096]{2,0,1:T(8,128)(2,1)} %copy.7), calls=%async_computation | async-start | bytes 8388608 | tf_op jit(solution)/shard_map/all_to_all | solution.py:16
  80.7 108.1 %all-gather.5.cloned.1.call-start = ((), (), s32[]{:S(2)}) async-start(), calls=%async_computation.3 | async-start | bytes 4718592 | tf_op jit(solution)/shard_map/all_gather | solution.py:20
  140.6 141.6 %reduce-scatter.2.cloned.1.call-start = ((), (), s32[]{:S(2)}) async-start(), calls=%async_computation.4 | async-start | bytes 4456448 | tf_op jit(solution)/shard_map/reduce_scatter | solution.py:25
Sparse Core Ops, SparseCore 0:
  11.1 55.7 all-gather.2
  140.7 48.0 all-gather.4
  204.1 78.0 reduce-scatter.1
where the time goes:
time: 290 us; the launch traced here: 289 us
  waiting for transfers between devices  233 us (80%)
  matrix products  20.9 us (7%)
  between operations  13.2 us (5%)
  local copies, waits for them, and re-layouts  10.5 us (4%)
  starting transfers between devices  7.48 us (3%)
  other arithmetic  3.26 us (1%)
    reduce_scatter x1, waiting for transfers between devices, local(): result = lax.psum_scatter(added, 'mod', scatter_dimension=0, tiled=True)  78.2 us
    all_gather x1, waiting for transfers between devices, local(): widened = lax.all_gather(slotted, 'ex', axis=0, tiled=True)  55.9 us
    all_to_all x1, waiting for transfers between devices, local(): lax.all_to_all(widened, 'mod', split_axis=1, concat_axis=0, tiled=True)  51 us
    all_gather x1, waiting for transfers between devices, local(): lax.all_gather(ordered, 'ex', axis=2, tiled=True)  48.2 us
    dot_general x1, matrix products, local(): lax.dot_general(lax.all_gather(ordered, 'ex', axis=2, tiled=True), train_...  15.1 us
    all_to_all x1, starting transfers between devices, local(): lax.all_to_all(widened, 'mod', split_axis=1, concat_axis=0, tiled=True)  7.4 us
    all_gather x1, local copies, waits for them, and re-layouts, local(): widened = lax.all_gather(slotted, 'ex', axis=0, tiled=True)  6.46 us
    dot_general x1, matrix products, precondition(): jnp.einsum('qmb,mab->qma', block, hessian_inv, preferred_element_type=jnp...  5.82 us
  transfers between devices with their start and end apart: 4, of which 4 were waited for; matrix products, arithmetic and copies ran while one was open for 0% of the time, Pallas kernels for 0%

commit v1 on v0

v1 whole, which is shorter than its diff:
```python
import jax
import jax.numpy as jnp
from jax import lax
from jax.experimental import pallas as pl
from jax.experimental.pallas import tpu as pltpu
from jax.sharding import PartitionSpec as P

AXES = ("mod", "ex")
NT = (((1,), (1,)), ((), ()))
VMEM = 12 * 1024 * 1024


def pairs(x=0, yl=0, z=0, yh=0, c=0, only=None):
    out = []
    for mod in range(16):
        for ex in range(8):
            if only is not None and mod % 2 not in only:
                continue
            core = mod % 2
            dyh = yh[core] if isinstance(yh, tuple) else yh
            to_mod = ((mod // 4 + z) % 4) * 4 + ((mod // 2 % 2) ^ dyh) * 2 + (core ^ c)
            to_ex = ((ex // 4) ^ yl) * 4 + (ex % 4 + x) % 4
            out.append((mod * 8 + ex, to_mod * 8 + to_ex))
    return out


def move(a, **offset):
    return lax.ppermute(a, AXES, pairs(**offset))


def spread(own):
    half = own.shape[0] // 2
    right = move(own, x=1)
    left = move(own, x=-1)
    across = move(own, yl=1)
    right, left, across = lax.optimization_barrier((right, left, across))
    far0 = move(right[:half], x=1)
    far1 = move(left[half:], x=-1)
    across_right = move(across, x=1)
    across_left = move(across, x=-1)
    corner0 = move(far0, yl=1)
    corner1 = move(far1, yl=1)
    return (own, right, left, across), (far0, far1, across_right, across_left, corner0, corner1)


def rows_of(blocks):
    return blocks[0][...] if len(blocks) == 1 else jnp.concatenate([b[...] for b in blocks], axis=0)


def on_chip(kernel, out_shape, scalars, *args):
    specs = [pl.BlockSpec(memory_space=pltpu.SMEM)] * len(scalars) + [pl.BlockSpec(memory_space=pltpu.VMEM)] * len(args)
    return pl.pallas_call(
        kernel,
        in_specs=specs,
        out_specs=pl.BlockSpec(memory_space=pltpu.VMEM),
        out_shape=out_shape,
        compiler_params=pltpu.CompilerParams(vmem_limit_bytes=VMEM),
        cost_estimate=pl.CostEstimate(flops=1, bytes_accessed=1, transcendentals=0),
    )(*scalars, *args)


def precondition(blocks, h):
    def kernel(*refs):
        *blocks, h, out = refs
        out[...] = lax.dot_general(rows_of(blocks), h[...], NT, preferred_element_type=jnp.float32).astype(out.dtype)

    rows = sum(b.shape[0] for b in blocks)
    return on_chip(kernel, jax.ShapeDtypeStruct((rows, 512), jnp.bfloat16), (), *blocks, h)


def precondition_order(blocks, h, first, place):
    def kernel(*refs):
        *blocks, h, first, place, out = refs
        rest = lax.dot_general(rows_of(blocks), h[...], NT, preferred_element_type=jnp.float32).astype(out.dtype)
        both = jnp.concatenate([first[...], rest], axis=0)
        at = lax.broadcasted_iota(jnp.int32, (512, 512), 0)
        pick = (place[...] == at).astype(both.dtype)
        out[...] = lax.dot_general(
            pick, both, (((0,), (0,)), ((), ())), preferred_element_type=jnp.float32
        ).astype(out.dtype)

    return on_chip(kernel, jax.ShapeDtypeStruct((512, 512), jnp.bfloat16), (), *blocks, h, first, place)


def score_near(blocks, near_slots, far_slots, sketch):
    total, tile = sketch.shape[0], 1024
    steps = total // tile

    def kernel(near_slots, far_slots, *refs):
        blocks, sketch, out, later, now, now_sem, later_sem = refs[:4], *refs[4:]

        def columns(slots, j):
            return pl.ds(pl.multiple_of(slots[j] * 512, 512), 512)

        fetch = [
            [
                pltpu.make_async_copy(
                    sketch.at[pl.ds(i * tile, tile), columns(near_slots, j)],
                    now.at[j, pl.ds(i * tile, tile)],
                    now_sem.at[i, j],
                )
                for j in range(4)
            ]
            for i in range(steps)
        ]
        ahead = [
            pltpu.make_async_copy(sketch.at[:, columns(far_slots, j)], later.at[j], later_sem.at[j]) for j in range(4)
        ]
        for copy in sum(fetch, []) + ahead:
            copy.start()
        for i in range(steps):
            terms = []
            for j in range(4):
                fetch[i][j].wait()
                terms.append(
                    lax.dot_general(
                        blocks[j][...], now[j, i * tile : i * tile + tile], NT, preferred_element_type=jnp.float32
                    )
                )
            out[:, i * tile : i * tile + tile] = sum(terms[1:], terms[0])
        for copy in ahead:
            copy.wait()

    smem, vmem = pl.BlockSpec(memory_space=pltpu.SMEM), pl.BlockSpec(memory_space=pltpu.VMEM)
    return pl.pallas_call(
        kernel,
        in_specs=[smem, smem, vmem, vmem, vmem, vmem, pl.BlockSpec(memory_space=pl.ANY)],
        out_specs=[vmem, vmem],
        out_shape=[
            jax.ShapeDtypeStruct((512, total), jnp.float32),
            jax.ShapeDtypeStruct((4, total, 512), jnp.bfloat16),
        ],
        scratch_shapes=[
            pltpu.VMEM((4, total, 512), jnp.bfloat16),
            pltpu.SemaphoreType.DMA((steps, 4)),
            pltpu.SemaphoreType.DMA((4,)),
        ],
        compiler_params=pltpu.CompilerParams(vmem_limit_bytes=2 * VMEM),
        cost_estimate=pl.CostEstimate(flops=1, bytes_accessed=1, transcendentals=0),
    )(near_slots, far_slots, *blocks, sketch)


def score_far(blocks, sketch, half, dtype, base, tile=1024):
    total = sketch.shape[1]

    def part(ref, columns=slice(None)):
        if ref.shape[0] == 256:
            return ref[:, columns]
        return ref[half * 256 : half * 256 + 256, columns]

    def kernel(*refs):
        blocks, sketch, base, out = refs[:4], *refs[4:]
        for i in range(total // tile):
            at = slice(i * tile, i * tile + tile)
            terms = [
                lax.dot_general(part(blocks[j]), sketch[j, at], NT, preferred_element_type=jnp.float32)
                for j in range(4)
            ]
            out[:, at] = sum(terms, part(base, at)).astype(out.dtype)

    return on_chip(kernel, jax.ShapeDtypeStruct((256, total), dtype), (), *blocks, sketch, base)


def local(queries, hessian_inv, train_sketch, module_slot, arrival_of):
    mod, ex = lax.axis_index("mod"), lax.axis_index("ex")
    z, yh, c = mod // 4, mod // 2 % 2, mod % 2
    yl, x = ex // 4, ex % 4
    h, sketch = hessian_inv[0], train_sketch[:, 0]

    pick = (module_slot[:, None] == jnp.arange(16)[None, :]).astype(jnp.bfloat16)
    slotted = jnp.einsum("km,rmb->krb", pick, queries, preferred_element_type=jnp.float32).astype(jnp.bfloat16)
    own = lax.all_to_all(slotted, "mod", split_axis=0, concat_axis=0, tiled=True).reshape(64, 4096)

    arrival = arrival_of.reshape(4, 2, 2, 32)
    arrival = lax.dynamic_slice_in_dim(jnp.concatenate([arrival, arrival], axis=0), z, 4, axis=0)
    yhs = [jnp.where(yh == c, arrival[:, 1 - s], arrival[:, s]) for s in (0, 1)]
    row = jnp.stack([jnp.where(c == 0, yhs[s], yhs[s][:, ::-1]) for s in (0, 1)])
    row = jnp.stack([row[0], row[1][:, ::-1]]).reshape(1, 512)
    source = row // 4 % 8
    dx, dy = (source % 4 - x) % 4, (source // 4) ^ yl
    block = jnp.where(
        dy == 0,
        jnp.where(dx == 0, 0, jnp.where(dx == 3, 1, jnp.where(dx == 1, 2, 4))),
        jnp.where(dx == 0, 3, jnp.where(dx == 3, 5, jnp.where(dx == 1, 6, 7))),
    )
    place = block * 64 + (row // 32) * 4 + row % 4
    left, right, over = (x + 3) % 4, (x + 1) % 4, (x + 2) % 4
    here, there = yl * 4, (1 - yl) * 4
    near_slots = jnp.stack([here + x, here + left, here + right, there + x]).astype(jnp.int32)
    far_slots = jnp.stack([here + over, there + left, there + right, there + over]).astype(jnp.int32)
    own, place, near_slots, far_slots = lax.optimization_barrier((own, place, near_slots, far_slots))

    near, far = spread(own)
    first = precondition(near, h)
    ordered = precondition_order(far, h, first, place)

    near, far = spread(ordered)
    base, later = score_near(near, near_slots, far_slots, sketch)
    far0, far1, across_right, across_left, corner0, corner1 = lax.optimization_barrier(far)
    send = score_far((far0, across_right, across_left, corner0), later, 0, jnp.bfloat16, base)
    got = move(send, c=1)
    keep = score_far((far1, across_right, across_left, corner1), later, 1, jnp.float32, base)

    chip = keep + got.astype(jnp.float32)
    parts = chip.astype(jnp.bfloat16)
    arrived = [move(parts[64 * d : 64 * d + 64], z=d, yh=(0, 1)) for d in (1, 2, 3)]
    other = move(parts[:64], yh=(0, 1), only=(1,))
    total = jnp.where(c == 0, chip[:64], other.astype(jnp.float32))
    for a in arrived:
        total = total + a.astype(jnp.float32)
    return total[32:] + move(total[:32], c=1)


def solution(mesh):
    in_specs = (P(("mod", "ex"), None, None), P("mod", "ex", None), P("ex", "mod", None), P(), P())
    out_specs = P("mod", "ex")
    return jax.shard_map(local, mesh=mesh, in_specs=in_specs, out_specs=out_specs, check_vma=False)
```

time: 290 us -> 126 us (0.43)
  waiting for transfers between devices: 233 us -> 57.9 us
  starting transfers between devices: 7.48 us -> 45.1 us
  matrix products: 20.9 us -> 1 us
  Pallas kernels: 0 us -> 14.9 us
  between operations: 13.2 us -> 0.29 us
  local copies, waits for them, and re-layouts: 10.5 us -> 4.97 us
    all_gather x2 -> x0, waiting for transfers between devices: 104 us -> none  [the longest x1 55.9 us: local(): widened = lax.all_gather(slotted, 'ex', axis=0, tiled=True)]
    reduce_scatter x1 -> x0, waiting for transfers between devices: 78.2 us -> none  [local(): result = lax.psum_scatter(added, 'mod', scatter_dimension=0, tiled=True)]
    ppermute x0 -> x24, waiting for transfers between devices: none -> 47.1 us  [move(): return lax.ppermute(a, AXES, pairs(**offset))]
    all_to_all x1, waiting for transfers between devices: 51 us -> 10.7 us  [local(): lax.all_to_all(slotted, 'mod', split_axis=0, concat_axis=0, tiled=True)]
    ppermute x0 -> x24, starting transfers between devices: none -> 35.6 us  [move(): return lax.ppermute(a, AXES, pairs(**offset))]
    dot_general x2 -> x1, matrix products: 20.9 us -> 1 us  [local(): jnp.einsum('km,rmb->krb', pick, queries, preferred_element_type=jnp.float32)]
    pallas_call x0 -> x5, Pallas kernels: none -> 14.9 us  [the longest x4 7.53 us: on_chip(): pl.pallas_call(kernel, in_specs=specs, out_specs=pl.BlockSpec(memory_spac...]
    all_gather x1 -> x0, local copies, waits for them, and re-layouts: 6.46 us -> none  [local(): widened = lax.all_gather(slotted, 'ex', axis=0, tiled=True)]
  transfers between devices with their start and end apart: 4 -> 25, of which waited for: 4 -> 19; matrix products, arithmetic and copies ran while one was open for 0% -> 0% of each run, Pallas kernels for 0% -> 9%
where the time goes in v1:
time: 126 us
  waiting for transfers between devices  57.9 us (46%)
  starting transfers between devices  45.1 us (36%)
  Pallas kernels  14.9 us (12%)
  local copies, waits for them, and re-layouts  4.97 us (4%)
  other arithmetic  1.55 us (1%)
    ppermute x24, waiting for transfers between devices, move(): return lax.ppermute(a, AXES, pairs(**offset))  47.1 us
    ppermute x24, starting transfers between devices, move(): return lax.ppermute(a, AXES, pairs(**offset))  35.6 us
    all_to_all x1, waiting for transfers between devices, local(): lax.all_to_all(slotted, 'mod', split_axis=0, concat_axis=0, tiled=True)  10.7 us
    all_to_all x1, starting transfers between devices, local(): lax.all_to_all(slotted, 'mod', split_axis=0, concat_axis=0, tiled=True)  9.46 us
    pallas_call x4, Pallas kernels, on_chip(): pl.pallas_call(kernel, in_specs=specs, out_specs=pl.BlockSpec(memory_spac...  7.53 us
    pallas_call x1, Pallas kernels, score_near(): pl.pallas_call(kernel, in_specs=[smem, smem, vmem, vmem, vmem, vmem, pl.B...  7.36 us
    unnamed x8, local copies, waits for them, and re-layouts  3.23 us
  transfers between devices with their start and end apart: 25, of which 19 were waited for; matrix products, arithmetic and copies ran while one was open for 0% of the time, Pallas kernels for 9%

profile of v1, /device:TPU:1, one launch (start us, length us, event | category | flops | bytes accessed | tf_op | source)
XLA Modules:
  0.0 125.6 jit_solution(4961026314537312472)
XLA Ops:
  3.2 9.5 %all-to-all-start = ((bf16[16,4,4096]{2,1,0:T(4,128)(2,1)}), bf16[16,4,4096]{2,1,0:T(4,128)(2,1)S(1)}, u32[]{:S(2)}, u32[]{:S(2)}) async-start(bf16[16,4,4096]{2,1,0:T(4,128)(2,1)} %copy.12), calls=%async_computation | async-start | bytes 1048576 | tf_op jit(solution)/shard_map/all_to_all | solution.py:172
  13.3 10.7 %all-to-all-done = bf16[16,4,4096]{2,1,0:T(4,128)(2,1)S(1)} async-done(((bf16[16,4,4096]{2,1,0:T(4,128)(2,1)}), bf16[16,4,4096]{2,1,0:T(4,128)(2,1)S(1)}, u32[]{:S(2)}, u32[]{:S(2)}) %all-to-all-start) | async-done | bytes 524320 | tf_op jit(solution)/shard_map/all_to_all | solution.py:172
  24.6 2.5 %collective-permute-start.1 = (bf16[64,4096]{1,0:T(8,128)(2,1)S(1)}, bf16[64,4096]{1,0:T(8,128)(2,1)S(1)}, u32[]{:S(2)}, u32[]{:S(2)}) collective-permute-start(bf16[64,4096]{1,0:T(8,128)(2,1)S(1)} %reshape.441.refs_0_), channel_id=1, source_target_pairs={{0,3},{1,0},{2,1},{3,2},{4,7},{5,4},{6,5},{7,6},{8,11},{9,8},{10,9... | collective-permute-start | bytes 1572872 | tf_op jit(solution)/shard_map/ppermute | solution.py:28
  27.1 9.4 %collective-permute-done.2.refs_3_ = bf16[64,4096]{1,0:T(8,128)(2,1)S(1)} collective-permute-done((bf16[64,4096]{1,0:T(8,128)(2,1)S(1)}, bf16[64,4096]{1,0:T(8,128)(2,1)S(1)}, u32[]{:S(2)}, u32[]{:S(2)}) %collective-permute-start.2) | collective-permute-done | bytes 524320 | tf_op jit(solution)/shard_map/ppermute | solution.py:28
  36.9 3.1 %collective-permute-done.refs_1_ = bf16[64,4096]{1,0:T(8,128)(2,1)S(1)} collective-permute-done((bf16[64,4096]{1,0:T(8,128)(2,1)S(1)}, bf16[64,4096]{1,0:T(8,128)(2,1)S(1)}, u32[]{:S(2)}, u32[]{:S(2)}) %collective-permute-start) | collective-permute-done | bytes 524320 | tf_op jit(solution)/shard_map/ppermute | solution.py:28
  40.1 2.7 %collective-permute-start.4 = (bf16[32,4096]{1,0:T(8,128)(2,1)S(1)}, bf16[32,4096]{1,0:T(8,128)(2,1)S(1)}, u32[]{:S(2)}, u32[]{:S(2)}) collective-permute-start(bf16[32,4096]{1,0:T(8,128)(2,1)S(1)} %slice.44), channel_id=1, source_target_pairs={{0,3},{1,0},{2,1},{3,2},{4,7},{5,4},{6,5},{7,6},{8,11},{9,8},{10,9... | collective-permute-start | bytes 786440 | tf_op jit(solution)/shard_map/ppermute | solution.py:28
  44.3 2.2 %collective-permute-done.3.refs_0_ = bf16[32,4096]{1,0:T(8,128)(2,1)S(1)} collective-permute-done((bf16[32,4096]{1,0:T(8,128)(2,1)S(1)}, bf16[32,4096]{1,0:T(8,128)(2,1)S(1)}, u32[]{:S(2)}, u32[]{:S(2)}) %collective-permute-start.3) | collective-permute-done | bytes 262176 | tf_op jit(solution)/shard_map/ppermute | solution.py:28
  48.0 2.2 %copy-done.1 = bf16[1,512,4096]{2,1,0:T(8,128)(2,1)S(1)} copy-done((bf16[1,512,4096]{2,1,0:T(8,128)(2,1)S(1)}, bf16[1,512,4096]{2,1,0:T(8,128)(2,1)}, u32[]{:S(2)}) %copy-start.1) | copy-done | bytes 4194328
  52.0 2.8 %collective-permute-done.8.refs_5_ = bf16[32,4096]{1,0:T(8,128)(2,1)S(1)} collective-permute-done((bf16[32,4096]{1,0:T(8,128)(2,1)S(1)}, bf16[32,4096]{1,0:T(8,128)(2,1)S(1)}, u32[]{:S(2)}, u32[]{:S(2)}) %collective-permute-start.8) | collective-permute-done | bytes 262176 | tf_op jit(solution)/shard_map/ppermute | solution.py:28
  54.8 1.9 %collective-permute-done.6.refs_3_ = bf16[64,4096]{1,0:T(8,128)(2,1)S(1)} collective-permute-done((bf16[64,4096]{1,0:T(8,128)(2,1)S(1)}, bf16[64,4096]{1,0:T(8,128)(2,1)S(1)}, u32[]{:S(2)}, u32[]{:S(2)}) %collective-permute-start.6) | collective-permute-done | bytes 524320 | tf_op jit(solution)/shard_map/ppermute | solution.py:28
  60.5 2.3 %collective-permute-start.10 = (bf16[512,512]{1,0:T(8,128)(2,1)S(1)}, bf16[512,512]{1,0:T(8,128)(2,1)S(1)}, u32[]{:S(2)}, u32[]{:S(2)}) collective-permute-start(bf16[512,512]{1,0:T(8,128)(2,1)S(1)} %shard_map.56.refs_0_), channel_id=1, source_target_pairs={{0,3},{1,0},{2,1},{3,2},{4,7},{5,4},{6,5},{7,6},{8,11},{9,8},{10,9... | collective-permute-start | bytes 1572872 | tf_op jit(solution)/shard_map/ppermute | solution.py:28
  62.9 5.5 %collective-permute-done.11.refs_3_ = bf16[512,512]{1,0:T(8,128)(2,1)S(1)} collective-permute-done((bf16[512,512]{1,0:T(8,128)(2,1)S(1)}, bf16[512,512]{1,0:T(8,128)(2,1)S(1)}, u32[]{:S(2)}, u32[]{:S(2)}) %collective-permute-start.11) | collective-permute-done | bytes 524320 | tf_op jit(solution)/shard_map/ppermute | solution.py:28
  70.0 3.1 %collective-permute-done.9.refs_1_ = bf16[512,512]{1,0:T(8,128)(2,1)S(1)} collective-permute-done((bf16[512,512]{1,0:T(8,128)(2,1)S(1)}, bf16[512,512]{1,0:T(8,128)(2,1)S(1)}, u32[]{:S(2)}, u32[]{:S(2)}) %collective-permute-start.9) | collective-permute-done | bytes 524320 | tf_op jit(solution)/shard_map/ppermute | solution.py:28
  76.2 2.3 %collective-permute-done.13.refs_0_ = bf16[256,512]{1,0:T(8,128)(2,1)S(1)} collective-permute-done((bf16[256,512]{1,0:T(8,128)(2,1)S(1)}, bf16[256,512]{1,0:T(8,128)(2,1)S(1)}, u32[]{:S(2)}, u32[]{:S(2)}) %collective-permute-start.13) | collective-permute-done | bytes 262176 | tf_op jit(solution)/shard_map/ppermute | solution.py:28
  78.9 1.6 %collective-permute-done.12.refs_0_ = bf16[256,512]{1,0:T(8,128)(2,1)S(1)} collective-permute-done((bf16[256,512]{1,0:T(8,128)(2,1)S(1)}, bf16[256,512]{1,0:T(8,128)(2,1)S(1)}, u32[]{:S(2)}, u32[]{:S(2)}) %collective-permute-start.12) | collective-permute-done | bytes 262176 | tf_op jit(solution)/shard_map/ppermute | solution.py:28
  80.9 7.4 %shard_map.57 = (f32[512,2048]{1,0:T(8,128)S(1)}, bf16[4,2048,512]{2,1,0:T(8,128)(2,1)S(1)}) custom-call(s32[4]{0:T(128)S(1)} %get-tuple-element.35.near_slots, s32[4]{0:T(128)S(1)} %get-tuple-element.36.far_slots, bf16[512,512]{1,0:T(8,128)(2,1)S(1)} %shard_map.56.refs_0_, bf16[512,512]{1,0:T(8,128)(2,1)S(1)} %collective-permute-done.9.refs_1_, ...), custom_call_target="tpu_custom_call" | custom-call | flops 1 | bytes 1 | tf_op jit(solution)/shard_map/pallas_call | solution.py:125
  89.0 2.4 %shard_map.59 = bf16[256,2048]{1,0:T(8,128)(2,1)S(1)} custom-call(bf16[256,512]{1,0:T(8,128)(2,1)S(1)} %collective-permute-done.12.refs_0_, bf16[512,512]{1,0:T(8,128)(2,1)S(1)} %collective-permute-done.14.refs_1_, bf16[512,512]{1,0:T(8,128)(2,1)S(1)} %collective-permute-done.15.refs_2_, bf16[256,512]{1,0:T(8,128)(2,1)S(1)} %collective-permute-done.16.refs_3_, ...), custom_call_target="tpu_custom_call" | custom-call | flops 1 | bytes 1 | tf_op jit(solution)/shard_map/pallas_call | solution.py:52
  91.4 8.8 %collective-permute-start.18 = (bf16[256,2048]{1,0:T(8,128)(2,1)S(1)}, bf16[256,2048]{1,0:T(8,128)(2,1)S(1)}, u32[]{:S(2)}, u32[]{:S(2)}) collective-permute-start(bf16[256,2048]{1,0:T(8,128)(2,1)S(1)} %shard_map.59), channel_id=1, source_target_pairs={{0,8},{1,9},{2,10},{3,11},{4,12},{5,13},{6,14},{7,15},{8,0},{9,1},... | collective-permute-start | bytes 3145736 | tf_op jit(solution)/shard_map/ppermute | solution.py:28
  100.2 2.4 %shard_map.58 = f32[256,2048]{1,0:T(8,128)S(1)} custom-call(bf16[256,512]{1,0:T(8,128)(2,1)S(1)} %collective-permute-done.13.refs_0_, bf16[512,512]{1,0:T(8,128)(2,1)S(1)} %collective-permute-done.14.refs_1_, bf16[512,512]{1,0:T(8,128)(2,1)S(1)} %collective-permute-done.15.refs_2_, bf16[256,512]{1,0:T(8,128)(2,1)S(1)} %collective-permute-done.17.refs_3_, ...), custom_call_target="tpu_custom_call" | custom-call | flops 1 | bytes 1 | tf_op jit(solution)/shard_map/pallas_call | solution.py:52
  103.1 5.1 %collective-permute-start.19 = (bf16[64,2048]{1,0:T(8,128)(2,1)S(1)}, bf16[64,2048]{1,0:T(8,128)(2,1)S(1)}, u32[]{:S(2)}, u32[]{:S(2)}) collective-permute-start(bf16[64,2048]{1,0:T(8,128)(2,1)S(1)} %get-tuple-element.43), channel_id=1, source_target_pairs={{8,24},{9,25},{10,26},{11,27},{12,28},{13,29},{14,30},{15,31},{24,... | collective-permute-start | bytes 786440 | tf_op jit(solution)/shard_map/ppermute | solution.py:28
  108.4 5.3 %collective-permute-start.21 = (bf16[64,2048]{1,0:T(8,128)(2,1)S(1)}, bf16[64,2048]{1,0:T(8,128)(2,1)S(1)}, u32[]{:S(2)}, u32[]{:S(2)}) collective-permute-start(bf16[64,2048]{1,0:T(8,128)(2,1)S(1)} %get-tuple-element.45), channel_id=1, source_target_pairs={{0,64},{1,65},{2,66},{3,67},{4,68},{5,69},{6,70},{7,71},{8,88},{9,... | collective-permute-start | bytes 786440 | tf_op jit(solution)/shard_map/ppermute | solution.py:28
  113.7 2.2 %collective-permute-done.22 = bf16[64,2048]{1,0:T(8,128)(2,1)S(1)} collective-permute-done((bf16[64,2048]{1,0:T(8,128)(2,1)S(1)}, bf16[64,2048]{1,0:T(8,128)(2,1)S(1)}, u32[]{:S(2)}, u32[]{:S(2)}) %collective-permute-start.22) | collective-permute-done | bytes 262176 | tf_op jit(solution)/shard_map/ppermute | solution.py:28
  115.9 4.9 %collective-permute-done.21 = bf16[64,2048]{1,0:T(8,128)(2,1)S(1)} collective-permute-done((bf16[64,2048]{1,0:T(8,128)(2,1)S(1)}, bf16[64,2048]{1,0:T(8,128)(2,1)S(1)}, u32[]{:S(2)}, u32[]{:S(2)}) %collective-permute-start.21) | collective-permute-done | bytes 262176 | tf_op jit(solution)/shard_map/ppermute | solution.py:28
  120.8 2.3 %collective-permute-done.20 = bf16[64,2048]{1,0:T(8,128)(2,1)S(1)} collective-permute-done((bf16[64,2048]{1,0:T(8,128)(2,1)S(1)}, bf16[64,2048]{1,0:T(8,128)(2,1)S(1)}, u32[]{:S(2)}, u32[]{:S(2)}) %collective-permute-start.20) | collective-permute-done | bytes 262176 | tf_op jit(solution)/shard_map/ppermute | solution.py:28
  (64 shorter events, 22.8 us)
Async XLA Ops:
  3.2 20.8 %all-to-all-start = ((bf16[16,4,4096]{2,1,0:T(4,128)(2,1)}), bf16[16,4,4096]{2,1,0:T(4,128)(2,1)S(1)}, u32[]{:S(2)}, u32[]{:S(2)}) async-start(bf16[16,4,4096]{2,1,0:T(4,128)(2,1)} %copy.12), calls=%async_computation | async-start | bytes 1048576 | tf_op jit(solution)/shard_map/all_to_all | solution.py:172
  24.1 12.3 %collective-permute-start.2 = (bf16[64,4096]{1,0:T(8,128)(2,1)S(1)}, bf16[64,4096]{1,0:T(8,128)(2,1)S(1)}, u32[]{:S(2)}, u32[]{:S(2)}) collective-permute-start(bf16[64,4096]{1,0:T(8,128)(2,1)S(1)} %reshape.441.refs_0_), channel_id=1, source_target_pairs={{0,4},{1,5},{2,6},{3,7},{4,0},{5,1},{6,2},{7,3},{8,12},{9,13},{10,... | collective-permute-start | bytes 1572872 | tf_op jit(solution)/shard_map/ppermute | solution.py:28
  24.6 12.2 %collective-permute-start.1 = (bf16[64,4096]{1,0:T(8,128)(2,1)S(1)}, bf16[64,4096]{1,0:T(8,128)(2,1)S(1)}, u32[]{:S(2)}, u32[]{:S(2)}) collective-permute-start(bf16[64,4096]{1,0:T(8,128)(2,1)S(1)} %reshape.441.refs_0_), channel_id=1, source_target_pairs={{0,3},{1,0},{2,1},{3,2},{4,7},{5,4},{6,5},{7,6},{8,11},{9,8},{10,9... | collective-permute-start | bytes 1572872 | tf_op jit(solution)/shard_map/ppermute | solution.py:28
  27.1 12.9 %collective-permute-start = (bf16[64,4096]{1,0:T(8,128)(2,1)S(1)}, bf16[64,4096]{1,0:T(8,128)(2,1)S(1)}, u32[]{:S(2)}, u32[]{:S(2)}) collective-permute-start(bf16[64,4096]{1,0:T(8,128)(2,1)S(1)} %reshape.441.refs_0_), channel_id=1, source_target_pairs={{0,1},{1,2},{2,3},{3,0},{4,5},{5,6},{6,7},{7,4},{8,9},{9,10},{10,1... | collective-permute-start | bytes 1572872 | tf_op jit(solution)/shard_map/ppermute | solution.py:28
  40.0 6.5 %collective-permute-start.3 = (bf16[32,4096]{1,0:T(8,128)(2,1)S(1)}, bf16[32,4096]{1,0:T(8,128)(2,1)S(1)}, u32[]{:S(2)}, u32[]{:S(2)}) collective-permute-start(bf16[32,4096]{1,0:T(8,128)(2,1)S(1)} %slice.43), channel_id=1, source_target_pairs={{0,1},{1,2},{2,3},{3,0},{4,5},{5,6},{6,7},{7,4},{8,9},{9,10},{10,1... | collective-permute-start | bytes 786440 | tf_op jit(solution)/shard_map/ppermute | solution.py:28
  40.1 7.5 %collective-permute-start.4 = (bf16[32,4096]{1,0:T(8,128)(2,1)S(1)}, bf16[32,4096]{1,0:T(8,128)(2,1)S(1)}, u32[]{:S(2)}, u32[]{:S(2)}) collective-permute-start(bf16[32,4096]{1,0:T(8,128)(2,1)S(1)} %slice.44), channel_id=1, source_target_pairs={{0,3},{1,0},{2,1},{3,2},{4,7},{5,4},{6,5},{7,6},{8,11},{9,8},{10,9... | collective-permute-start | bytes 786440 | tf_op jit(solution)/shard_map/ppermute | solution.py:28
  42.9 13.9 %collective-permute-start.6 = (bf16[64,4096]{1,0:T(8,128)(2,1)S(1)}, bf16[64,4096]{1,0:T(8,128)(2,1)S(1)}, u32[]{:S(2)}, u32[]{:S(2)}) collective-permute-start(bf16[64,4096]{1,0:T(8,128)(2,1)S(1)} %collective-permute-done.2.refs_3_), channel_id=1, source_target_pairs={{0,3},{1,0},{2,1},{3,2},{4,7},{5,4},{6,5},{7,6},{8,11},{9,8},{10,9... | collective-permute-start | bytes 1572872 | tf_op jit(solution)/shard_map/ppermute | solution.py:28
  42.9 14.9 %collective-permute-start.5 = (bf16[64,4096]{1,0:T(8,128)(2,1)S(1)}, bf16[64,4096]{1,0:T(8,128)(2,1)S(1)}, u32[]{:S(2)}, u32[]{:S(2)}) collective-permute-start(bf16[64,4096]{1,0:T(8,128)(2,1)S(1)} %collective-permute-done.2.refs_3_), channel_id=1, source_target_pairs={{0,1},{1,2},{2,3},{3,0},{4,5},{5,6},{6,7},{7,4},{8,9},{9,10},{10,1... | collective-permute-start | bytes 1572872 | tf_op jit(solution)/shard_map/ppermute | solution.py:28
  46.5 5.5 %collective-permute-start.7 = (bf16[32,4096]{1,0:T(8,128)(2,1)S(1)}, bf16[32,4096]{1,0:T(8,128)(2,1)S(1)}, u32[]{:S(2)}, u32[]{:S(2)}) collective-permute-start(bf16[32,4096]{1,0:T(8,128)(2,1)S(1)} %collective-permute-done.3.refs_0_), channel_id=1, source_target_pairs={{0,4},{1,5},{2,6},{3,7},{4,0},{5,1},{6,2},{7,3},{8,12},{9,13},{10,... | collective-permute-start | bytes 786440 | tf_op jit(solution)/shard_map/ppermute | solution.py:28
  47.6 7.3 %collective-permute-start.8 = (bf16[32,4096]{1,0:T(8,128)(2,1)S(1)}, bf16[32,4096]{1,0:T(8,128)(2,1)S(1)}, u32[]{:S(2)}, u32[]{:S(2)}) collective-permute-start(bf16[32,4096]{1,0:T(8,128)(2,1)S(1)} %collective-permute-done.4.refs_1_), channel_id=1, source_target_pairs={{0,4},{1,5},{2,6},{3,7},{4,0},{5,1},{6,2},{7,3},{8,12},{9,13},{10,... | collective-permute-start | bytes 786440 | tf_op jit(solution)/shard_map/ppermute | solution.py:28
  59.4 9.0 %collective-permute-start.11 = (bf16[512,512]{1,0:T(8,128)(2,1)S(1)}, bf16[512,512]{1,0:T(8,128)(2,1)S(1)}, u32[]{:S(2)}, u32[]{:S(2)}) collective-permute-start(bf16[512,512]{1,0:T(8,128)(2,1)S(1)} %shard_map.56.refs_0_), channel_id=1, source_target_pairs={{0,4},{1,5},{2,6},{3,7},{4,0},{5,1},{6,2},{7,3},{8,12},{9,13},{10,... | collective-permute-start | bytes 1572872 | tf_op jit(solution)/shard_map/ppermute | solution.py:28
  60.5 9.4 %collective-permute-start.10 = (bf16[512,512]{1,0:T(8,128)(2,1)S(1)}, bf16[512,512]{1,0:T(8,128)(2,1)S(1)}, u32[]{:S(2)}, u32[]{:S(2)}) collective-permute-start(bf16[512,512]{1,0:T(8,128)(2,1)S(1)} %shard_map.56.refs_0_), channel_id=1, source_target_pairs={{0,3},{1,0},{2,1},{3,2},{4,7},{5,4},{6,5},{7,6},{8,11},{9,8},{10,9... | collective-permute-start | bytes 1572872 | tf_op jit(solution)/shard_map/ppermute | solution.py:28
  62.9 10.2 %collective-permute-start.9 = (bf16[512,512]{1,0:T(8,128)(2,1)S(1)}, bf16[512,512]{1,0:T(8,128)(2,1)S(1)}, u32[]{:S(2)}, u32[]{:S(2)}) collective-permute-start(bf16[512,512]{1,0:T(8,128)(2,1)S(1)} %shard_map.56.refs_0_), channel_id=1, source_target_pairs={{0,1},{1,2},{2,3},{3,0},{4,5},{5,6},{6,7},{7,4},{8,9},{9,10},{10,1... | collective-permute-start | bytes 1572872 | tf_op jit(solution)/shard_map/ppermute | solution.py:28
  73.1 5.4 %collective-permute-start.13 = (bf16[256,512]{1,0:T(8,128)(2,1)S(1)}, bf16[256,512]{1,0:T(8,128)(2,1)S(1)}, u32[]{:S(2)}, u32[]{:S(2)}) collective-permute-start(bf16[256,512]{1,0:T(8,128)(2,1)S(1)} %slice.46), channel_id=1, source_target_pairs={{0,3},{1,0},{2,1},{3,2},{4,7},{5,4},{6,5},{7,6},{8,11},{9,8},{10,9... | collective-permute-start | bytes 786440 | tf_op jit(solution)/shard_map/ppermute | solution.py:28
  73.5 7.1 %collective-permute-start.12 = (bf16[256,512]{1,0:T(8,128)(2,1)S(1)}, bf16[256,512]{1,0:T(8,128)(2,1)S(1)}, u32[]{:S(2)}, u32[]{:S(2)}) collective-permute-start(bf16[256,512]{1,0:T(8,128)(2,1)S(1)} %slice.45), channel_id=1, source_target_pairs={{0,1},{1,2},{2,3},{3,0},{4,5},{5,6},{6,7},{7,4},{8,9},{9,10},{10,1... | collective-permute-start | bytes 786440 | tf_op jit(solution)/shard_map/ppermute | solution.py:28
  74.7 13.6 %collective-permute-start.15 = (bf16[512,512]{1,0:T(8,128)(2,1)S(1)}, bf16[512,512]{1,0:T(8,128)(2,1)S(1)}, u32[]{:S(2)}, u32[]{:S(2)}) collective-permute-start(bf16[512,512]{1,0:T(8,128)(2,1)S(1)} %collective-permute-done.11.refs_3_), channel_id=1, source_target_pairs={{0,3},{1,0},{2,1},{3,2},{4,7},{5,4},{6,5},{7,6},{8,11},{9,8},{10,9... | collective-permute-start | bytes 1572872 | tf_op jit(solution)/shard_map/ppermute | solution.py:28
  76.2 12.8 %collective-permute-start.14 = (bf16[512,512]{1,0:T(8,128)(2,1)S(1)}, bf16[512,512]{1,0:T(8,128)(2,1)S(1)}, u32[]{:S(2)}, u32[]{:S(2)}) collective-permute-start(bf16[512,512]{1,0:T(8,128)(2,1)S(1)} %collective-permute-done.11.refs_3_), channel_id=1, source_target_pairs={{0,1},{1,2},{2,3},{3,0},{4,5},{5,6},{6,7},{7,4},{8,9},{9,10},{10,1... | collective-permute-start | bytes 1572872 | tf_op jit(solution)/shard_map/ppermute | solution.py:28
  78.5 9.8 %collective-permute-start.17 = (bf16[256,512]{1,0:T(8,128)(2,1)S(1)}, bf16[256,512]{1,0:T(8,128)(2,1)S(1)}, u32[]{:S(2)}, u32[]{:S(2)}) collective-permute-start(bf16[256,512]{1,0:T(8,128)(2,1)S(1)} %collective-permute-done.13.refs_0_), channel_id=1, source_target_pairs={{0,4},{1,5},{2,6},{3,7},{4,0},{5,1},{6,2},{7,3},{8,12},{9,13},{10,... | collective-permute-start | bytes 786440 | tf_op jit(solution)/shard_map/ppermute | solution.py:28
  80.5 7.8 %collective-permute-start.16 = (bf16[256,512]{1,0:T(8,128)(2,1)S(1)}, bf16[256,512]{1,0:T(8,128)(2,1)S(1)}, u32[]{:S(2)}, u32[]{:S(2)}) collective-permute-start(bf16[256,512]{1,0:T(8,128)(2,1)S(1)} %collective-permute-done.12.refs_0_), channel_id=1, source_target_pairs={{0,4},{1,5},{2,6},{3,7},{4,0},{5,1},{6,2},{7,3},{8,12},{9,13},{10,... | collective-permute-start | bytes 786440 | tf_op jit(solution)/shard_map/ppermute | solution.py:28
  91.4 11.2 %collective-permute-start.18 = (bf16[256,2048]{1,0:T(8,128)(2,1)S(1)}, bf16[256,2048]{1,0:T(8,128)(2,1)S(1)}, u32[]{:S(2)}, u32[]{:S(2)}) collective-permute-start(bf16[256,2048]{1,0:T(8,128)(2,1)S(1)} %shard_map.59), channel_id=1, source_target_pairs={{0,8},{1,9},{2,10},{3,11},{4,12},{5,13},{6,14},{7,15},{8,0},{9,1},... | collective-permute-start | bytes 3145736 | tf_op jit(solution)/shard_map/ppermute | solution.py:28
  103.1 10.6 %collective-permute-start.19 = (bf16[64,2048]{1,0:T(8,128)(2,1)S(1)}, bf16[64,2048]{1,0:T(8,128)(2,1)S(1)}, u32[]{:S(2)}, u32[]{:S(2)}) collective-permute-start(bf16[64,2048]{1,0:T(8,128)(2,1)S(1)} %get-tuple-element.43), channel_id=1, source_target_pairs={{8,24},{9,25},{10,26},{11,27},{12,28},{13,29},{14,30},{15,31},{24,... | collective-permute-start | bytes 786440 | tf_op jit(solution)/shard_map/ppermute | solution.py:28
  108.2 7.7 %collective-permute-start.22 = (bf16[64,2048]{1,0:T(8,128)(2,1)S(1)}, bf16[64,2048]{1,0:T(8,128)(2,1)S(1)}, u32[]{:S(2)}, u32[]{:S(2)}) collective-permute-start(bf16[64,2048]{1,0:T(8,128)(2,1)S(1)} %get-tuple-element.44), channel_id=1, source_target_pairs={{0,96},{1,97},{2,98},{3,99},{4,100},{5,101},{6,102},{7,103},{8,120... | collective-permute-start | bytes 786440 | tf_op jit(solution)/shard_map/ppermute | solution.py:28
  108.4 12.4 %collective-permute-start.21 = (bf16[64,2048]{1,0:T(8,128)(2,1)S(1)}, bf16[64,2048]{1,0:T(8,128)(2,1)S(1)}, u32[]{:S(2)}, u32[]{:S(2)}) collective-permute-start(bf16[64,2048]{1,0:T(8,128)(2,1)S(1)} %get-tuple-element.45), channel_id=1, source_target_pairs={{0,64},{1,65},{2,66},{3,67},{4,68},{5,69},{6,70},{7,71},{8,88},{9,... | collective-permute-start | bytes 786440 | tf_op jit(solution)/shard_map/ppermute | solution.py:28
  113.7 9.4 %collective-permute-start.20 = (bf16[64,2048]{1,0:T(8,128)(2,1)S(1)}, bf16[64,2048]{1,0:T(8,128)(2,1)S(1)}, u32[]{:S(2)}, u32[]{:S(2)}) collective-permute-start(bf16[64,2048]{1,0:T(8,128)(2,1)S(1)} %get-tuple-element.46), channel_id=1, source_target_pairs={{0,32},{1,33},{2,34},{3,35},{4,36},{5,37},{6,38},{7,39},{8,56},{9,... | collective-permute-start | bytes 786440 | tf_op jit(solution)/shard_map/ppermute | solution.py:28
  (5 other events, 25.2 us)

commit v2 on v1

v2 whole, which is shorter than its diff:
```python
import jax
import jax.numpy as jnp
from jax import lax
from jax.experimental import pallas as pl
from jax.experimental.pallas import tpu as pltpu
from jax.sharding import PartitionSpec as P

AXES = ("mod", "ex")
NT = (((1,), (1,)), ((), ()))
VMEM = 12 * 1024 * 1024


def pairs(x=0, yl=0, z=0, yh=0, c=0, only=None):
    out = []
    for mod in range(16):
        for ex in range(8):
            if only is not None and mod % 2 not in only:
                continue
            core = mod % 2
            dyh = yh[core] if isinstance(yh, tuple) else yh
            to_mod = ((mod // 4 + z) % 4) * 4 + ((mod // 2 % 2) ^ dyh) * 2 + (core ^ c)
            to_ex = ((ex // 4) ^ yl) * 4 + (ex % 4 + x) % 4
            out.append((mod * 8 + ex, to_mod * 8 + to_ex))
    return out


def move(a, **offset):
    return lax.ppermute(a, AXES, pairs(**offset))


def spread(top, low, meanwhile=None):
    across = move(jnp.concatenate([top, low], axis=0), yl=1)
    right_top, left_low = move(top, x=1), move(low, x=-1)
    right_low, left_top = move(low, x=1), move(top, x=-1)
    right_top, left_low, meanwhile = lax.optimization_barrier((right_top, left_low, meanwhile))
    far0, far1 = move(right_top, x=1), move(left_low, x=-1)
    across, right_low, left_top = lax.optimization_barrier((across, right_low, left_top))
    across_right, across_left = move(across, x=1), move(across, x=-1)
    corner0, corner1 = move(far0, yl=1), move(far1, yl=1)
    near = (top, low, right_top, right_low, left_top, left_low, across)
    return near, (far0, far1, across_right, across_left, corner0, corner1), meanwhile


def rows_of(blocks):
    return blocks[0][...] if len(blocks) == 1 else jnp.concatenate([b[...] for b in blocks], axis=0)


def on_chip(kernel, out_shape, scalars, *args):
    specs = [pl.BlockSpec(memory_space=pltpu.SMEM)] * len(scalars) + [pl.BlockSpec(memory_space=pltpu.VMEM)] * len(args)
    return pl.pallas_call(
        kernel,
        in_specs=specs,
        out_specs=jax.tree.map(lambda _: pl.BlockSpec(memory_space=pltpu.VMEM), out_shape),
        out_shape=out_shape,
        compiler_params=pltpu.CompilerParams(vmem_limit_bytes=VMEM),
        cost_estimate=pl.CostEstimate(flops=1, bytes_accessed=1, transcendentals=0),
    )(*scalars, *args)


def precondition(blocks, h):
    def kernel(*refs):
        *blocks, h, out = refs
        out[...] = lax.dot_general(rows_of(blocks), h[...], NT, preferred_element_type=jnp.float32).astype(out.dtype)

    rows = sum(b.shape[0] for b in blocks)
    return on_chip(kernel, jax.ShapeDtypeStruct((rows, 512), jnp.bfloat16), (), *blocks, h)


def precondition_order(blocks, h, first, place):
    def kernel(*refs):
        *blocks, h, first, place, top, low = refs
        rest = lax.dot_general(rows_of(blocks), h[...], NT, preferred_element_type=jnp.float32).astype(top.dtype)
        both = jnp.concatenate([first[...], rest], axis=0)
        at = lax.broadcasted_iota(jnp.int32, (512, 512), 0)
        pick = (place[...] == at).astype(both.dtype)
        ordered = lax.dot_general(pick, both, (((0,), (0,)), ((), ())), preferred_element_type=jnp.float32)
        top[...] = ordered[:256].astype(top.dtype)
        low[...] = ordered[256:].astype(low.dtype)

    half = jax.ShapeDtypeStruct((256, 512), jnp.bfloat16)
    return on_chip(kernel, [half, half], (), *blocks, h, first, place)


def score_own(top, low, slots, sketch):
    total, tile = sketch.shape[0], 1024
    steps = total // tile

    def kernel(slots, top, low, sketch, out, later, now, now_sem, later_sem):
        def columns(j):
            return pl.ds(pl.multiple_of(slots[j] * 512, 512), 512)

        fetch = [
            pltpu.make_async_copy(
                sketch.at[pl.ds(i * tile, tile), columns(0)], now.at[pl.ds(i * tile, tile)], now_sem.at[i]
            )
            for i in range(steps)
        ]
        ahead = [pltpu.make_async_copy(sketch.at[:, columns(j + 1)], later.at[j], later_sem.at[j]) for j in range(7)]
        for copy in fetch + ahead:
            copy.start()
        rows = rows_of((top, low))
        for i in range(steps):
            fetch[i].wait()
            at = slice(i * tile, i * tile + tile)
            out[:, at] = lax.dot_general(rows, now[at], NT, preferred_element_type=jnp.float32)
        for copy in ahead:
            copy.wait()

    smem, vmem = pl.BlockSpec(memory_space=pltpu.SMEM), pl.BlockSpec(memory_space=pltpu.VMEM)
    return pl.pallas_call(
        kernel,
        in_specs=[smem, vmem, vmem, pl.BlockSpec(memory_space=pl.ANY)],
        out_specs=[vmem, vmem],
        out_shape=[
            jax.ShapeDtypeStruct((512, total), jnp.float32),
            jax.ShapeDtypeStruct((7, total, 512), jnp.bfloat16),
        ],
        scratch_shapes=[
            pltpu.VMEM((total, 512), jnp.bfloat16),
            pltpu.SemaphoreType.DMA((steps,)),
            pltpu.SemaphoreType.DMA((7,)),
        ],
        compiler_params=pltpu.CompilerParams(vmem_limit_bytes=28 * 1024 * 1024),
        cost_estimate=pl.CostEstimate(flops=1, bytes_accessed=1, transcendentals=0),
    )(slots, top, low, sketch)


def score_more(blocks, first, sketch, base, half=None, dtype=jnp.float32, tile=1024):
    total = sketch.shape[1]
    sizes = [len(b) for b in blocks]
    rows = 512 if half is None else 256

    def part(ref, columns=slice(None)):
        if ref.shape[0] == rows:
            return ref[:, columns]
        return ref[half * 256 : half * 256 + 256, columns]

    def kernel(*refs):
        held, (sketch, base, out) = list(refs[:-3]), refs[-3:]
        wholes = []
        for size in sizes:
            taken = [held.pop(0) for _ in range(size)]
            wholes.append(rows_of(taken) if size > 1 else part(taken[0]))
        for i in range(total // tile):
            at = slice(i * tile, i * tile + tile)
            terms = [
                lax.dot_general(w, sketch[first + j, at], NT, preferred_element_type=jnp.float32)
                for j, w in enumerate(wholes)
            ]
            out[:, at] = sum(terms, part(base, at)).astype(out.dtype)

    flat = [a for b in blocks for a in b]
    return on_chip(kernel, jax.ShapeDtypeStruct((rows, total), dtype), (), *flat, sketch, base)


def local(queries, hessian_inv, train_sketch, module_slot, arrival_of):
    mod, ex = lax.axis_index("mod"), lax.axis_index("ex")
    z, yh, c = mod // 4, mod // 2 % 2, mod % 2
    yl, x = ex // 4, ex % 4
    h, sketch = hessian_inv[0], train_sketch[:, 0]

    pick = (module_slot[:, None] == jnp.arange(16)[None, :]).astype(jnp.bfloat16)
    slotted = jnp.einsum("km,rmb->krb", pick, queries, preferred_element_type=jnp.float32).astype(jnp.bfloat16)
    own = lax.all_to_all(slotted, "mod", split_axis=0, concat_axis=0, tiled=True).reshape(64, 4096)

    arrival = arrival_of.reshape(4, 2, 2, 32)
    arrival = lax.dynamic_slice_in_dim(jnp.concatenate([arrival, arrival], axis=0), z, 4, axis=0)
    yhs = [jnp.where(yh == c, arrival[:, 1 - s], arrival[:, s]) for s in (0, 1)]
    row = jnp.stack([jnp.where(c == 0, yhs[s], yhs[s][:, ::-1]) for s in (0, 1)])
    row = jnp.stack([row[0], row[1][:, ::-1]]).reshape(1, 512)
    source = row // 4 % 8
    dx, dy = (source % 4 - x) % 4, (source // 4) ^ yl
    block = jnp.where(
        dy == 0,
        jnp.where(dx == 0, 0, jnp.where(dx == 3, 1, jnp.where(dx == 1, 2, 4))),
        jnp.where(dx == 0, 3, jnp.where(dx == 3, 5, jnp.where(dx == 1, 6, 7))),
    )
    place = block * 64 + (row // 32) * 4 + row % 4
    left, right, over = (x + 3) % 4, (x + 1) % 4, (x + 2) % 4
    here, there = yl * 4, (1 - yl) * 4
    slots = [here + x, here + left, here + right, there + x, here + over, there + left, there + right, there + over]
    own, place, slots = lax.optimization_barrier((own, place, jnp.stack(slots).astype(jnp.int32)))

    near, far, _ = spread(own[:32], own[32:])
    first = precondition(near, h)
    top, low = precondition_order(far, h, first, place)

    near, far, (base, later) = spread(top, low, score_own(top, low, slots, sketch))
    _, _, right_top, right_low, left_top, left_low, across = near
    far0, far1, *far = far
    base = score_more(((right_top, right_low), (left_top, left_low), (across,), (far0, far1)), 0, later, base)
    across_right, across_left, corner0, corner1 = lax.optimization_barrier(far)
    send = score_more(((across_right,), (across_left,), (corner0,)), 4, later, base, 0, jnp.bfloat16)
    got = move(send, c=1)
    keep = score_more(((across_right,), (across_left,), (corner1,)), 4, later, base, 1)

    chip = keep + got.astype(jnp.float32)
    parts = chip.astype(jnp.bfloat16)
    arrived = [move(parts[64 * d : 64 * d + 64], z=d, yh=(0, 1)) for d in (1, 2, 3)]
    other = move(parts[:64], yh=(0, 1), only=(1,))
    total = jnp.where(c == 0, chip[:64], other.astype(jnp.float32))
    for a in arrived:
        total = total + a.astype(jnp.float32)
    return total[32:] + move(total[:32], c=1)


def solution(mesh):
    in_specs = (P(("mod", "ex"), None, None), P("mod", "ex", None), P("ex", "mod", None), P(), P())
    out_specs = P("mod", "ex")
    return jax.shard_map(local, mesh=mesh, in_specs=in_specs, out_specs=out_specs, check_vma=False)
```

time: 126 us -> 119 us (0.944)
  waiting for transfers between devices: 57.9 us -> 38.7 us
  starting transfers between devices: 45.1 us -> 54.6 us
  Pallas kernels: 14.9 us -> 17.6 us
    ppermute x24 -> x28, waiting for transfers between devices: 47.1 us -> 27.9 us  [move(): return lax.ppermute(a, AXES, pairs(**offset))]
    ppermute x24 -> x28, starting transfers between devices: 35.6 us -> 45.1 us  [move(): return lax.ppermute(a, AXES, pairs(**offset))]
    pallas_call x5 -> x6, Pallas kernels: 14.9 us -> 17.6 us  [the longest x5 11 us: on_chip(): pl.pallas_call(kernel, in_specs=specs, out_specs=jax.tree.map(lambda _: p...]
  transfers between devices with their start and end apart: 25 -> 29, of which waited for: 19 -> 16; matrix products, arithmetic and copies ran while one was open for 0% -> 0% of each run, Pallas kernels for 9% -> 12%
where the time goes in v2:
time: 119 us
  starting transfers between devices  54.6 us (46%)
  waiting for transfers between devices  38.7 us (33%)
  Pallas kernels  17.6 us (15%)
  local copies, waits for them, and re-layouts  5.02 us (4%)
  other arithmetic  1.43 us (1%)
    ppermute x28, starting transfers between devices, move(): return lax.ppermute(a, AXES, pairs(**offset))  45.1 us
    ppermute x28, waiting for transfers between devices, move(): return lax.ppermute(a, AXES, pairs(**offset))  27.9 us
    pallas_call x5, Pallas kernels, on_chip(): pl.pallas_call(kernel, in_specs=specs, out_specs=jax.tree.map(lambda _: p...  11 us
    all_to_all x1, waiting for transfers between devices, local(): lax.all_to_all(slotted, 'mod', split_axis=0, concat_axis=0, tiled=True)  10.8 us
    all_to_all x1, starting transfers between devices, local(): lax.all_to_all(slotted, 'mod', split_axis=0, concat_axis=0, tiled=True)  9.46 us
    pallas_call x1, Pallas kernels, score_own(): pl.pallas_call(kernel, in_specs=[smem, vmem, vmem, pl.BlockSpec(memory_sp...  6.59 us
    unnamed x8, local copies, waits for them, and re-layouts  3.23 us
  transfers between devices with their start and end apart: 29, of which 16 were waited for; matrix products, arithmetic and copies ran while one was open for 0% of the time, Pallas kernels for 12%

profile of v2, /device:TPU:1, one launch (start us, length us, event | category | flops | bytes accessed | tf_op | source)
XLA Modules:
  0.0 118.5 jit_solution(3764813090712466409)
XLA Ops:
  3.2 9.5 %all-to-all-start = ((bf16[16,4,4096]{2,1,0:T(4,128)(2,1)}), bf16[16,4,4096]{2,1,0:T(4,128)(2,1)S(1)}, u32[]{:S(2)}, u32[]{:S(2)}) async-start(bf16[16,4,4096]{2,1,0:T(4,128)(2,1)} %copy.12), calls=%async_computation | async-start | bytes 1048576 | tf_op jit(solution)/shard_map/all_to_all | solution.py:164
  13.2 10.8 %all-to-all-done = bf16[16,4,4096]{2,1,0:T(4,128)(2,1)S(1)} async-done(((bf16[16,4,4096]{2,1,0:T(4,128)(2,1)}), bf16[16,4,4096]{2,1,0:T(4,128)(2,1)S(1)}, u32[]{:S(2)}, u32[]{:S(2)}) %all-to-all-start) | async-done | bytes 524320 | tf_op jit(solution)/shard_map/all_to_all | solution.py:164
  27.4 2.7 %collective-permute-start.6 = (bf16[32,4096]{1,0:T(8,128)(2,1)S(1)}, bf16[32,4096]{1,0:T(8,128)(2,1)S(1)}, u32[]{:S(2)}, u32[]{:S(2)}) collective-permute-start(bf16[32,4096]{1,0:T(8,128)(2,1)S(1)} %get-tuple-element.58.refs_0_), channel_id=1, source_target_pairs={{0,3},{1,0},{2,1},{3,2},{4,7},{5,4},{6,5},{7,6},{8,11},{9,8},{10,9... | collective-permute-start | bytes 786440 | tf_op jit(solution)/shard_map/ppermute | solution.py:28
  30.1 2.2 %collective-permute-done.refs_2_ = bf16[32,4096]{1,0:T(8,128)(2,1)S(1)} collective-permute-done((bf16[32,4096]{1,0:T(8,128)(2,1)S(1)}, bf16[32,4096]{1,0:T(8,128)(2,1)S(1)}, u32[]{:S(2)}, u32[]{:S(2)}) %collective-permute-start) | collective-permute-done | bytes 262176 | tf_op jit(solution)/shard_map/ppermute | solution.py:28
  32.3 2.4 %collective-permute-start.3 = (bf16[32,4096]{1,0:T(8,128)(2,1)S(1)}, bf16[32,4096]{1,0:T(8,128)(2,1)S(1)}, u32[]{:S(2)}, u32[]{:S(2)}) collective-permute-start(bf16[32,4096]{1,0:T(8,128)(2,1)S(1)} %collective-permute-done.1.refs_5_), channel_id=1, source_target_pairs={{0,3},{1,0},{2,1},{3,2},{4,7},{5,4},{6,5},{7,6},{8,11},{9,8},{10,9... | collective-permute-start | bytes 786440 | tf_op jit(solution)/shard_map/ppermute | solution.py:28
  34.7 3.2 %collective-permute-done.5.refs_3_ = bf16[32,4096]{1,0:T(8,128)(2,1)S(1)} collective-permute-done((bf16[32,4096]{1,0:T(8,128)(2,1)S(1)}, bf16[32,4096]{1,0:T(8,128)(2,1)S(1)}, u32[]{:S(2)}, u32[]{:S(2)}) %collective-permute-start.5) | collective-permute-done | bytes 262176 | tf_op jit(solution)/shard_map/ppermute | solution.py:28
  40.6 2.7 %collective-permute-done.3.refs_1_ = bf16[32,4096]{1,0:T(8,128)(2,1)S(1)} collective-permute-done((bf16[32,4096]{1,0:T(8,128)(2,1)S(1)}, bf16[32,4096]{1,0:T(8,128)(2,1)S(1)}, u32[]{:S(2)}, u32[]{:S(2)}) %collective-permute-start.3) | collective-permute-done | bytes 262176 | tf_op jit(solution)/shard_map/ppermute | solution.py:28
  44.7 2.2 %copy-done.1 = bf16[1,512,4096]{2,1,0:T(8,128)(2,1)S(1)} copy-done((bf16[1,512,4096]{2,1,0:T(8,128)(2,1)S(1)}, bf16[1,512,4096]{2,1,0:T(8,128)(2,1)}, u32[]{:S(2)}) %copy-start.1) | copy-done | bytes 4194328
  48.8 3.0 %collective-permute-done.9.refs_4_ = bf16[32,4096]{1,0:T(8,128)(2,1)S(1)} collective-permute-done((bf16[32,4096]{1,0:T(8,128)(2,1)S(1)}, bf16[32,4096]{1,0:T(8,128)(2,1)S(1)}, u32[]{:S(2)}, u32[]{:S(2)}) %collective-permute-start.9) | collective-permute-done | bytes 262176 | tf_op jit(solution)/shard_map/ppermute | solution.py:28
  52.3 2.2 %collective-permute-done.8.refs_3_ = bf16[64,4096]{1,0:T(8,128)(2,1)S(1)} collective-permute-done((bf16[64,4096]{1,0:T(8,128)(2,1)S(1)}, bf16[64,4096]{1,0:T(8,128)(2,1)S(1)}, u32[]{:S(2)}, u32[]{:S(2)}) %collective-permute-start.8) | collective-permute-done | bytes 524320 | tf_op jit(solution)/shard_map/ppermute | solution.py:28
  59.9 2.7 %collective-permute-start.13 = (bf16[256,512]{1,0:T(8,128)(2,1)S(1)}, bf16[256,512]{1,0:T(8,128)(2,1)S(1)}, u32[]{:S(2)}, u32[]{:S(2)}) collective-permute-start(bf16[256,512]{1,0:T(8,128)(2,1)S(1)} %get-tuple-element.35.top), channel_id=1, source_target_pairs={{0,3},{1,0},{2,1},{3,2},{4,7},{5,4},{6,5},{7,6},{8,11},{9,8},{10,9... | collective-permute-start | bytes 786440 | tf_op jit(solution)/shard_map/ppermute | solution.py:28
  62.6 6.6 %shard_map.57 = (f32[512,2048]{1,0:T(8,128)S(1)}, bf16[7,2048,512]{2,1,0:T(8,128)(2,1)S(1)}) custom-call(s32[8]{0:T(128)S(1)} %stack.47.slots, bf16[256,512]{1,0:T(8,128)(2,1)S(1)} %get-tuple-element.35.top, bf16[256,512]{1,0:T(8,128)(2,1)S(1)} %get-tuple-element.36.low, bf16[2048,4096]{1,0:T(8,128)(2,1)} %bitcast.45), custom_call_target="tpu_custom_call" | custom-call | flops 1 | bytes 1 | tf_op jit(solution)/shard_map/pallas_call | solution.py:110
  69.3 2.7 %collective-permute-start.20 = (bf16[256,512]{1,0:T(8,128)(2,1)S(1)}, bf16[256,512]{1,0:T(8,128)(2,1)S(1)}, u32[]{:S(2)}, u32[]{:S(2)}) collective-permute-start(bf16[256,512]{1,0:T(8,128)(2,1)S(1)} %collective-permute-done.17.refs_3_), channel_id=1, source_target_pairs={{0,3},{1,0},{2,1},{3,2},{4,7},{5,4},{6,5},{7,6},{8,11},{9,8},{10,9... | collective-permute-start | bytes 786440 | tf_op jit(solution)/shard_map/ppermute | solution.py:28
  72.0 2.7 %collective-permute-start.15 = (bf16[512,512]{1,0:T(8,128)(2,1)S(1)}, bf16[512,512]{1,0:T(8,128)(2,1)S(1)}, u32[]{:S(2)}, u32[]{:S(2)}) collective-permute-start(bf16[512,512]{1,0:T(8,128)(2,1)S(1)} %collective-permute-done.11.refs_4_), channel_id=1, source_target_pairs={{0,3},{1,0},{2,1},{3,2},{4,7},{5,4},{6,5},{7,6},{8,11},{9,8},{10,9... | collective-permute-start | bytes 1572872 | tf_op jit(solution)/shard_map/ppermute | solution.py:28
  77.2 4.6 %shard_map.58.refs_4_ = f32[512,2048]{1,0:T(8,128)S(1)} custom-call(bf16[256,512]{1,0:T(8,128)(2,1)S(1)} %collective-permute-done.16.refs_0_, bf16[256,512]{1,0:T(8,128)(2,1)S(1)} %collective-permute-done.12.refs_1_, bf16[256,512]{1,0:T(8,128)(2,1)S(1)} %collective-permute-done.13.refs_2_, bf16[256,512]{1,0:T(8,128)(2,1)S(1)} %collective-permute-done.17.refs_3_, ...), custom_call_target="tpu_custom_call" | custom-call | flops 1 | bytes 1 | tf_op jit(solution)/shard_map/pallas_call | solution.py:50
  81.8 2.3 %collective-permute-done.21.refs_2_ = bf16[256,512]{1,0:T(8,128)(2,1)S(1)} collective-permute-done((bf16[256,512]{1,0:T(8,128)(2,1)S(1)}, bf16[256,512]{1,0:T(8,128)(2,1)S(1)}, u32[]{:S(2)}, u32[]{:S(2)}) %collective-permute-start.21) | collective-permute-done | bytes 262176 | tf_op jit(solution)/shard_map/ppermute | solution.py:28
  85.0 1.8 %shard_map.60 = bf16[256,2048]{1,0:T(8,128)(2,1)S(1)} custom-call(bf16[512,512]{1,0:T(8,128)(2,1)S(1)} %collective-permute-done.14.refs_0_, bf16[512,512]{1,0:T(8,128)(2,1)S(1)} %collective-permute-done.15.refs_1_, bf16[256,512]{1,0:T(8,128)(2,1)S(1)} %collective-permute-done.19.refs_2_, bf16[7,2048,512]{2,1,0:T(8,128)(2,1)S(1)} %get-tuple-element.46.refs_7_.refs_3_, ...), custom_call_target="tpu_custom_call" | custom-call | flops 1 | bytes 1 | tf_op jit(solution)/shard_map/pallas_call | solution.py:50
  86.8 8.5 %collective-permute-start.22 = (bf16[256,2048]{1,0:T(8,128)(2,1)S(1)}, bf16[256,2048]{1,0:T(8,128)(2,1)S(1)}, u32[]{:S(2)}, u32[]{:S(2)}) collective-permute-start(bf16[256,2048]{1,0:T(8,128)(2,1)S(1)} %shard_map.60), channel_id=1, source_target_pairs={{0,8},{1,9},{2,10},{3,11},{4,12},{5,13},{6,14},{7,15},{8,0},{9,1},... | collective-permute-start | bytes 3145736 | tf_op jit(solution)/shard_map/ppermute | solution.py:28
  98.1 4.0 %collective-permute-start.23 = (bf16[64,2048]{1,0:T(8,128)(2,1)S(1)}, bf16[64,2048]{1,0:T(8,128)(2,1)S(1)}, u32[]{:S(2)}, u32[]{:S(2)}) collective-permute-start(bf16[64,2048]{1,0:T(8,128)(2,1)S(1)} %get-tuple-element.53), channel_id=1, source_target_pairs={{8,24},{9,25},{10,26},{11,27},{12,28},{13,29},{14,30},{15,31},{24,... | collective-permute-start | bytes 786440 | tf_op jit(solution)/shard_map/ppermute | solution.py:28
  103.3 2.7 %collective-permute-start.25 = (bf16[64,2048]{1,0:T(8,128)(2,1)S(1)}, bf16[64,2048]{1,0:T(8,128)(2,1)S(1)}, u32[]{:S(2)}, u32[]{:S(2)}) collective-permute-start(bf16[64,2048]{1,0:T(8,128)(2,1)S(1)} %get-tuple-element.55), channel_id=1, source_target_pairs={{0,64},{1,65},{2,66},{3,67},{4,68},{5,69},{6,70},{7,71},{8,88},{9,... | collective-permute-start | bytes 786440 | tf_op jit(solution)/shard_map/ppermute | solution.py:28
  106.0 2.7 %collective-permute-start.26 = (bf16[64,2048]{1,0:T(8,128)(2,1)S(1)}, bf16[64,2048]{1,0:T(8,128)(2,1)S(1)}, u32[]{:S(2)}, u32[]{:S(2)}) collective-permute-start(bf16[64,2048]{1,0:T(8,128)(2,1)S(1)} %get-tuple-element.54), channel_id=1, source_target_pairs={{0,96},{1,97},{2,98},{3,99},{4,100},{5,101},{6,102},{7,103},{8,120... | collective-permute-start | bytes 786440 | tf_op jit(solution)/shard_map/ppermute | solution.py:28
  108.7 2.6 %collective-permute-done.24 = bf16[64,2048]{1,0:T(8,128)(2,1)S(1)} collective-permute-done((bf16[64,2048]{1,0:T(8,128)(2,1)S(1)}, bf16[64,2048]{1,0:T(8,128)(2,1)S(1)}, u32[]{:S(2)}, u32[]{:S(2)}) %collective-permute-start.24) | collective-permute-done | bytes 262176 | tf_op jit(solution)/shard_map/ppermute | solution.py:28
  111.3 2.6 %collective-permute-done.25 = bf16[64,2048]{1,0:T(8,128)(2,1)S(1)} collective-permute-done((bf16[64,2048]{1,0:T(8,128)(2,1)S(1)}, bf16[64,2048]{1,0:T(8,128)(2,1)S(1)}, u32[]{:S(2)}, u32[]{:S(2)}) %collective-permute-start.25) | collective-permute-done | bytes 262176 | tf_op jit(solution)/shard_map/ppermute | solution.py:28
  113.8 2.1 %collective-permute-done.26 = bf16[64,2048]{1,0:T(8,128)(2,1)S(1)} collective-permute-done((bf16[64,2048]{1,0:T(8,128)(2,1)S(1)}, bf16[64,2048]{1,0:T(8,128)(2,1)S(1)}, u32[]{:S(2)}, u32[]{:S(2)}) %collective-permute-start.26) | collective-permute-done | bytes 262176 | tf_op jit(solution)/shard_map/ppermute | solution.py:28
  (71 shorter events, 29.1 us)
Async XLA Ops:
  3.2 20.8 %all-to-all-start = ((bf16[16,4,4096]{2,1,0:T(4,128)(2,1)}), bf16[16,4,4096]{2,1,0:T(4,128)(2,1)S(1)}, u32[]{:S(2)}, u32[]{:S(2)}) async-start(bf16[16,4,4096]{2,1,0:T(4,128)(2,1)} %copy.12), calls=%async_computation | async-start | bytes 1048576 | tf_op jit(solution)/shard_map/all_to_all | solution.py:164
  24.1 13.8 %collective-permute-start.4 = (bf16[64,4096]{1,0:T(8,128)(2,1)S(1)}, bf16[64,4096]{1,0:T(8,128)(2,1)S(1)}, u32[]{:S(2)}, u32[]{:S(2)}) collective-permute-start(bf16[64,4096]{1,0:T(8,128)(2,1)S(1)} %reshape.441), channel_id=1, source_target_pairs={{0,4},{1,5},{2,6},{3,7},{4,0},{5,1},{6,2},{7,3},{8,12},{9,13},{10,... | collective-permute-start | bytes 1572872 | tf_op jit(solution)/shard_map/ppermute | solution.py:28
  24.7 7.6 %collective-permute-start = (bf16[32,4096]{1,0:T(8,128)(2,1)S(1)}, bf16[32,4096]{1,0:T(8,128)(2,1)S(1)}, u32[]{:S(2)}, u32[]{:S(2)}) collective-permute-start(bf16[32,4096]{1,0:T(8,128)(2,1)S(1)} %get-tuple-element.58.refs_0_), channel_id=1, source_target_pairs={{0,1},{1,2},{2,3},{3,0},{4,5},{5,6},{6,7},{7,4},{8,9},{9,10},{10,1... | collective-permute-start | bytes 786440 | tf_op jit(solution)/shard_map/ppermute | solution.py:28
  27.4 10.5 %collective-permute-start.5 = (bf16[32,4096]{1,0:T(8,128)(2,1)S(1)}, bf16[32,4096]{1,0:T(8,128)(2,1)S(1)}, u32[]{:S(2)}, u32[]{:S(2)}) collective-permute-start(bf16[32,4096]{1,0:T(8,128)(2,1)S(1)} %get-tuple-element.57.refs_1_), channel_id=1, source_target_pairs={{0,1},{1,2},{2,3},{3,0},{4,5},{5,6},{6,7},{7,4},{8,9},{9,10},{10,1... | collective-permute-start | bytes 786440 | tf_op jit(solution)/shard_map/ppermute | solution.py:28
  27.4 10.5 %collective-permute-start.6 = (bf16[32,4096]{1,0:T(8,128)(2,1)S(1)}, bf16[32,4096]{1,0:T(8,128)(2,1)S(1)}, u32[]{:S(2)}, u32[]{:S(2)}) collective-permute-start(bf16[32,4096]{1,0:T(8,128)(2,1)S(1)} %get-tuple-element.58.refs_0_), channel_id=1, source_target_pairs={{0,3},{1,0},{2,1},{3,2},{4,7},{5,4},{6,5},{7,6},{8,11},{9,8},{10,9... | collective-permute-start | bytes 786440 | tf_op jit(solution)/shard_map/ppermute | solution.py:28
  32.3 11.0 %collective-permute-start.3 = (bf16[32,4096]{1,0:T(8,128)(2,1)S(1)}, bf16[32,4096]{1,0:T(8,128)(2,1)S(1)}, u32[]{:S(2)}, u32[]{:S(2)}) collective-permute-start(bf16[32,4096]{1,0:T(8,128)(2,1)S(1)} %collective-permute-done.1.refs_5_), channel_id=1, source_target_pairs={{0,3},{1,0},{2,1},{3,2},{4,7},{5,4},{6,5},{7,6},{8,11},{9,8},{10,9... | collective-permute-start | bytes 786440 | tf_op jit(solution)/shard_map/ppermute | solution.py:28
  34.7 9.6 %collective-permute-start.2 = (bf16[32,4096]{1,0:T(8,128)(2,1)S(1)}, bf16[32,4096]{1,0:T(8,128)(2,1)S(1)}, u32[]{:S(2)}, u32[]{:S(2)}) collective-permute-start(bf16[32,4096]{1,0:T(8,128)(2,1)S(1)} %collective-permute-done.refs_2_), channel_id=1, source_target_pairs={{0,1},{1,2},{2,3},{3,0},{4,5},{5,6},{6,7},{7,4},{8,9},{9,10},{10,1... | collective-permute-start | bytes 786440 | tf_op jit(solution)/shard_map/ppermute | solution.py:28
  37.9 14.4 %collective-permute-start.7 = (bf16[64,4096]{1,0:T(8,128)(2,1)S(1)}, bf16[64,4096]{1,0:T(8,128)(2,1)S(1)}, u32[]{:S(2)}, u32[]{:S(2)}) collective-permute-start(bf16[64,4096]{1,0:T(8,128)(2,1)S(1)} %collective-permute-done.4.refs_6_), channel_id=1, source_target_pairs={{0,1},{1,2},{2,3},{3,0},{4,5},{5,6},{6,7},{7,4},{8,9},{9,10},{10,1... | collective-permute-start | bytes 1572872 | tf_op jit(solution)/shard_map/ppermute | solution.py:28
  38.8 15.6 %collective-permute-start.8 = (bf16[64,4096]{1,0:T(8,128)(2,1)S(1)}, bf16[64,4096]{1,0:T(8,128)(2,1)S(1)}, u32[]{:S(2)}, u32[]{:S(2)}) collective-permute-start(bf16[64,4096]{1,0:T(8,128)(2,1)S(1)} %collective-permute-done.4.refs_6_), channel_id=1, source_target_pairs={{0,3},{1,0},{2,1},{3,2},{4,7},{5,4},{6,5},{7,6},{8,11},{9,8},{10,9... | collective-permute-start | bytes 1572872 | tf_op jit(solution)/shard_map/ppermute | solution.py:28
  44.3 7.5 %collective-permute-start.9 = (bf16[32,4096]{1,0:T(8,128)(2,1)S(1)}, bf16[32,4096]{1,0:T(8,128)(2,1)S(1)}, u32[]{:S(2)}, u32[]{:S(2)}) collective-permute-start(bf16[32,4096]{1,0:T(8,128)(2,1)S(1)} %collective-permute-done.2.refs_0_), channel_id=1, source_target_pairs={{0,4},{1,5},{2,6},{3,7},{4,0},{5,1},{6,2},{7,3},{8,12},{9,13},{10,... | collective-permute-start | bytes 786440 | tf_op jit(solution)/shard_map/ppermute | solution.py:28
  56.1 15.9 %collective-permute-start.11 = (bf16[512,512]{1,0:T(8,128)(2,1)S(1)}, bf16[512,512]{1,0:T(8,128)(2,1)S(1)}, u32[]{:S(2)}, u32[]{:S(2)}) collective-permute-start(bf16[512,512]{1,0:T(8,128)(2,1)S(1)} %pad_maximum_fusion), channel_id=1, source_target_pairs={{0,4},{1,5},{2,6},{3,7},{4,0},{5,1},{6,2},{7,3},{8,12},{9,13},{10,... | collective-permute-start | bytes 1572872 | tf_op jit(solution)/shard_map/ppermute | solution.py:28
  57.2 12.0 %collective-permute-start.16 = (bf16[256,512]{1,0:T(8,128)(2,1)S(1)}, bf16[256,512]{1,0:T(8,128)(2,1)S(1)}, u32[]{:S(2)}, u32[]{:S(2)}) collective-permute-start(bf16[256,512]{1,0:T(8,128)(2,1)S(1)} %get-tuple-element.35.top), channel_id=1, source_target_pairs={{0,1},{1,2},{2,3},{3,0},{4,5},{5,6},{6,7},{7,4},{8,9},{9,10},{10,1... | collective-permute-start | bytes 786440 | tf_op jit(solution)/shard_map/ppermute | solution.py:28
  58.4 10.8 %collective-permute-start.17 = (bf16[256,512]{1,0:T(8,128)(2,1)S(1)}, bf16[256,512]{1,0:T(8,128)(2,1)S(1)}, u32[]{:S(2)}, u32[]{:S(2)}) collective-permute-start(bf16[256,512]{1,0:T(8,128)(2,1)S(1)} %get-tuple-element.36.low), channel_id=1, source_target_pairs={{0,3},{1,0},{2,1},{3,2},{4,7},{5,4},{6,5},{7,6},{8,11},{9,8},{10,9... | collective-permute-start | bytes 786440 | tf_op jit(solution)/shard_map/ppermute | solution.py:28
  59.9 12.0 %collective-permute-start.12 = (bf16[256,512]{1,0:T(8,128)(2,1)S(1)}, bf16[256,512]{1,0:T(8,128)(2,1)S(1)}, u32[]{:S(2)}, u32[]{:S(2)}) collective-permute-start(bf16[256,512]{1,0:T(8,128)(2,1)S(1)} %get-tuple-element.36.low), channel_id=1, source_target_pairs={{0,1},{1,2},{2,3},{3,0},{4,5},{5,6},{6,7},{7,4},{8,9},{9,10},{10,1... | collective-permute-start | bytes 786440 | tf_op jit(solution)/shard_map/ppermute | solution.py:28
  59.9 12.0 %collective-permute-start.13 = (bf16[256,512]{1,0:T(8,128)(2,1)S(1)}, bf16[256,512]{1,0:T(8,128)(2,1)S(1)}, u32[]{:S(2)}, u32[]{:S(2)}) collective-permute-start(bf16[256,512]{1,0:T(8,128)(2,1)S(1)} %get-tuple-element.35.top), channel_id=1, source_target_pairs={{0,3},{1,0},{2,1},{3,2},{4,7},{5,4},{6,5},{7,6},{8,11},{9,8},{10,9... | collective-permute-start | bytes 786440 | tf_op jit(solution)/shard_map/ppermute | solution.py:28
  69.3 6.8 %collective-permute-start.20 = (bf16[256,512]{1,0:T(8,128)(2,1)S(1)}, bf16[256,512]{1,0:T(8,128)(2,1)S(1)}, u32[]{:S(2)}, u32[]{:S(2)}) collective-permute-start(bf16[256,512]{1,0:T(8,128)(2,1)S(1)} %collective-permute-done.17.refs_3_), channel_id=1, source_target_pairs={{0,3},{1,0},{2,1},{3,2},{4,7},{5,4},{6,5},{7,6},{8,11},{9,8},{10,9... | collective-permute-start | bytes 786440 | tf_op jit(solution)/shard_map/ppermute | solution.py:28
  72.0 13.0 %collective-permute-start.14 = (bf16[512,512]{1,0:T(8,128)(2,1)S(1)}, bf16[512,512]{1,0:T(8,128)(2,1)S(1)}, u32[]{:S(2)}, u32[]{:S(2)}) collective-permute-start(bf16[512,512]{1,0:T(8,128)(2,1)S(1)} %collective-permute-done.11.refs_4_), channel_id=1, source_target_pairs={{0,1},{1,2},{2,3},{3,0},{4,5},{5,6},{6,7},{7,4},{8,9},{9,10},{10,1... | collective-permute-start | bytes 1572872 | tf_op jit(solution)/shard_map/ppermute | solution.py:28
  72.0 13.0 %collective-permute-start.15 = (bf16[512,512]{1,0:T(8,128)(2,1)S(1)}, bf16[512,512]{1,0:T(8,128)(2,1)S(1)}, u32[]{:S(2)}, u32[]{:S(2)}) collective-permute-start(bf16[512,512]{1,0:T(8,128)(2,1)S(1)} %collective-permute-done.11.refs_4_), channel_id=1, source_target_pairs={{0,3},{1,0},{2,1},{3,2},{4,7},{5,4},{6,5},{7,6},{8,11},{9,8},{10,9... | collective-permute-start | bytes 1572872 | tf_op jit(solution)/shard_map/ppermute | solution.py:28
  76.1 7.9 %collective-permute-start.21 = (bf16[256,512]{1,0:T(8,128)(2,1)S(1)}, bf16[256,512]{1,0:T(8,128)(2,1)S(1)}, u32[]{:S(2)}, u32[]{:S(2)}) collective-permute-start(bf16[256,512]{1,0:T(8,128)(2,1)S(1)} %collective-permute-done.20.refs_6_), channel_id=1, source_target_pairs={{0,4},{1,5},{2,6},{3,7},{4,0},{5,1},{6,2},{7,3},{8,12},{9,13},{10,... | collective-permute-start | bytes 786440 | tf_op jit(solution)/shard_map/ppermute | solution.py:28
  86.8 10.8 %collective-permute-start.22 = (bf16[256,2048]{1,0:T(8,128)(2,1)S(1)}, bf16[256,2048]{1,0:T(8,128)(2,1)S(1)}, u32[]{:S(2)}, u32[]{:S(2)}) collective-permute-start(bf16[256,2048]{1,0:T(8,128)(2,1)S(1)} %shard_map.60), channel_id=1, source_target_pairs={{0,8},{1,9},{2,10},{3,11},{4,12},{5,13},{6,14},{7,15},{8,0},{9,1},... | collective-permute-start | bytes 3145736 | tf_op jit(solution)/shard_map/ppermute | solution.py:28
  98.1 10.6 %collective-permute-start.23 = (bf16[64,2048]{1,0:T(8,128)(2,1)S(1)}, bf16[64,2048]{1,0:T(8,128)(2,1)S(1)}, u32[]{:S(2)}, u32[]{:S(2)}) collective-permute-start(bf16[64,2048]{1,0:T(8,128)(2,1)S(1)} %get-tuple-element.53), channel_id=1, source_target_pairs={{8,24},{9,25},{10,26},{11,27},{12,28},{13,29},{14,30},{15,31},{24,... | collective-permute-start | bytes 786440 | tf_op jit(solution)/shard_map/ppermute | solution.py:28
  102.1 9.2 %collective-permute-start.24 = (bf16[64,2048]{1,0:T(8,128)(2,1)S(1)}, bf16[64,2048]{1,0:T(8,128)(2,1)S(1)}, u32[]{:S(2)}, u32[]{:S(2)}) collective-permute-start(bf16[64,2048]{1,0:T(8,128)(2,1)S(1)} %get-tuple-element.56), channel_id=1, source_target_pairs={{0,32},{1,33},{2,34},{3,35},{4,36},{5,37},{6,38},{7,39},{8,56},{9,... | collective-permute-start | bytes 786440 | tf_op jit(solution)/shard_map/ppermute | solution.py:28
  103.3 10.5 %collective-permute-start.25 = (bf16[64,2048]{1,0:T(8,128)(2,1)S(1)}, bf16[64,2048]{1,0:T(8,128)(2,1)S(1)}, u32[]{:S(2)}, u32[]{:S(2)}) collective-permute-start(bf16[64,2048]{1,0:T(8,128)(2,1)S(1)} %get-tuple-element.55), channel_id=1, source_target_pairs={{0,64},{1,65},{2,66},{3,67},{4,68},{5,69},{6,70},{7,71},{8,88},{9,... | collective-permute-start | bytes 786440 | tf_op jit(solution)/shard_map/ppermute | solution.py:28
  106.0 9.9 %collective-permute-start.26 = (bf16[64,2048]{1,0:T(8,128)(2,1)S(1)}, bf16[64,2048]{1,0:T(8,128)(2,1)S(1)}, u32[]{:S(2)}, u32[]{:S(2)}) collective-permute-start(bf16[64,2048]{1,0:T(8,128)(2,1)S(1)} %get-tuple-element.54), channel_id=1, source_target_pairs={{0,96},{1,97},{2,98},{3,99},{4,100},{5,101},{6,102},{7,103},{8,120... | collective-permute-start | bytes 786440 | tf_op jit(solution)/shard_map/ppermute | solution.py:28
  (9 other events, 49.5 us)

commit v3 on v2

--- a/solution.py
+++ b/solution.py
@@ -28,8 +28,8 @@
     return lax.ppermute(a, AXES, pairs(**offset))
 
 
-def spread(top, low, meanwhile=None):
-    across = move(jnp.concatenate([top, low], axis=0), yl=1)
+def spread(top, low, whole, meanwhile=None):
+    across = move(whole, yl=1)
     right_top, left_low = move(top, x=1), move(low, x=-1)
     right_low, left_top = move(low, x=1), move(top, x=-1)
     right_top, left_low, meanwhile = lax.optimization_barrier((right_top, left_low, meanwhile))
@@ -68,7 +68,7 @@
 
 def precondition_order(blocks, h, first, place):
     def kernel(*refs):
-        *blocks, h, first, place, top, low = refs
+        *blocks, h, first, place, top, low, whole = refs
         rest = lax.dot_general(rows_of(blocks), h[...], NT, preferred_element_type=jnp.float32).astype(top.dtype)
         both = jnp.concatenate([first[...], rest], axis=0)
         at = lax.broadcasted_iota(jnp.int32, (512, 512), 0)
@@ -76,53 +76,47 @@
         ordered = lax.dot_general(pick, both, (((0,), (0,)), ((), ())), preferred_element_type=jnp.float32)
         top[...] = ordered[:256].astype(top.dtype)
         low[...] = ordered[256:].astype(low.dtype)
+        whole[...] = ordered.astype(low.dtype)
 
     half = jax.ShapeDtypeStruct((256, 512), jnp.bfloat16)
-    return on_chip(kernel, [half, half], (), *blocks, h, first, place)
-
-
-def score_own(top, low, slots, sketch):
+    return on_chip(kernel, [half, half, jax.ShapeDtypeStruct((512, 512), jnp.bfloat16)], (), *blocks, h, first, place)
+
+
+def columns_of(slots, first, count, sketch, limit, top=None, low=None, held=None):
     total, tile = sketch.shape[0], 1024
-    steps = total // tile
-
-    def kernel(slots, top, low, sketch, out, later, now, now_sem, later_sem):
-        def columns(j):
-            return pl.ds(pl.multiple_of(slots[j] * 512, 512), 512)
-
-        fetch = [
+
+    def kernel(slots, sketch, *refs):
+        later, sems = refs[-2:]
+        copies = [
             pltpu.make_async_copy(
-                sketch.at[pl.ds(i * tile, tile), columns(0)], now.at[pl.ds(i * tile, tile)], now_sem.at[i]
+                sketch.at[:, pl.ds(pl.multiple_of(slots[first + j] * 512, 512), 512)], later.at[j], sems.at[j]
             )
-            for i in range(steps)
+            for j in range(count)
         ]
-        ahead = [pltpu.make_async_copy(sketch.at[:, columns(j + 1)], later.at[j], later_sem.at[j]) for j in range(7)]
-        for copy in fetch + ahead:
+        for copy in copies:
             copy.start()
-        rows = rows_of((top, low))
-        for i in range(steps):
-            fetch[i].wait()
-            at = slice(i * tile, i * tile + tile)
-            out[:, at] = lax.dot_general(rows, now[at], NT, preferred_element_type=jnp.float32)
-        for copy in ahead:
+        if top is not None:
+            top_ref, low_ref, held_ref, out = refs[:4]
+            rows = rows_of((top_ref, low_ref))
+            for i in range(total // tile):
+                at = slice(i * tile, i * tile + tile)
+                out[:, at] = lax.dot_general(rows, held_ref[0, at], NT, preferred_element_type=jnp.float32)
+        for copy in copies:
             copy.wait()
 
     smem, vmem = pl.BlockSpec(memory_space=pltpu.SMEM), pl.BlockSpec(memory_space=pltpu.VMEM)
+    args = () if top is None else (top, low, held)
+    out = [] if top is None else [jax.ShapeDtypeStruct((512, total), jnp.float32)]
+    out += [jax.ShapeDtypeStruct((count, total, 512), jnp.bfloat16)]
     return pl.pallas_call(
         kernel,
-        in_specs=[smem, vmem, vmem, pl.BlockSpec(memory_space=pl.ANY)],
-        out_specs=[vmem, vmem],
-        out_shape=[
-            jax.ShapeDtypeStruct((512, total), jnp.float32),
-            jax.ShapeDtypeStruct((7, total, 512), jnp.bfloat16),
-        ],
-        scratch_shapes=[
-            pltpu.VMEM((total, 512), jnp.bfloat16),
-            pltpu.SemaphoreType.DMA((steps,)),
-            pltpu.SemaphoreType.DMA((7,)),
-        ],
-        compiler_params=pltpu.CompilerParams(vmem_limit_bytes=28 * 1024 * 1024),
+        in_specs=[smem, pl.BlockSpec(memory_space=pl.ANY)] + [vmem] * len(args),
+        out_specs=[vmem] * len(out),
+        out_shape=out,
+        scratch_shapes=[pltpu.SemaphoreType.DMA((count,))],
+        compiler_params=pltpu.CompilerParams(vmem_limit_bytes=limit * 1024 * 1024),
         cost_estimate=pl.CostEstimate(flops=1, bytes_accessed=1, transcendentals=0),
-    )(slots, top, low, sketch)
+    )(slots, sketch, *args)
 
 
 def score_more(blocks, first, sketch, base, half=None, dtype=jnp.float32, tile=1024):
@@ -181,18 +175,20 @@
     slots = [here + x, here + left, here + right, there + x, here + over, there + left, there + right, there + over]
     own, place, slots = lax.optimization_barrier((own, place, jnp.stack(slots).astype(jnp.int32)))
 
-    near, far, _ = spread(own[:32], own[32:])
+    near, far, _ = spread(own[:32], own[32:], own)
     first = precondition(near, h)
-    top, low = precondition_order(far, h, first, place)
-
-    near, far, (base, later) = spread(top, low, score_own(top, low, slots, sketch))
+    (now,) = columns_of(slots, 0, 5, sketch, 28)
+    far, first, now = lax.optimization_barrier((far, first, now))
+    top, low, whole = precondition_order(far, h, first, place)
+
+    near, far, (base, later) = spread(top, low, whole, columns_of(slots, 5, 3, sketch, 28, top, low, now))
     _, _, right_top, right_low, left_top, left_low, across = near
     far0, far1, *far = far
-    base = score_more(((right_top, right_low), (left_top, left_low), (across,), (far0, far1)), 0, later, base)
+    base = score_more(((right_top, right_low), (left_top, left_low), (across,), (far0, far1)), 1, now, base)
     across_right, across_left, corner0, corner1 = lax.optimization_barrier(far)
-    send = score_more(((across_right,), (across_left,), (corner0,)), 4, later, base, 0, jnp.bfloat16)
+    send = score_more(((across_right,), (across_left,), (corner0,)), 0, later, base, 0, jnp.bfloat16)
     got = move(send, c=1)
-    keep = score_more(((across_right,), (across_left,), (corner1,)), 4, later, base, 1)
+    keep = score_more(((across_right,), (across_left,), (corner1,)), 0, later, base, 1)
 
     chip = keep + got.astype(jnp.float32)
     parts = chip.astype(jnp.bfloat16)

time: 119 us -> 117 us (0.983)
  starting transfers between devices: 54.6 us -> 51.1 us
  Pallas kernels: 17.6 us -> 20.6 us
    ppermute x28, starting transfers between devices: 45.1 us -> 41.6 us  [move(): return lax.ppermute(a, AXES, pairs(**offset))]
    pallas_call x1 -> x2, Pallas kernels: 6.59 us -> 9.42 us  [columns_of(): pl.pallas_call(kernel, in_specs=[smem, pl.BlockSpec(memory_space=pl.ANY)]...]
    unnamed x8 -> x6, local copies, waits for them, and re-layouts: 3.23 us -> 1.39 us
  transfers between devices with their start and end apart: 29 -> 29, of which waited for: 16 -> 16; matrix products, arithmetic and copies ran while one was open for 0% -> 1% of each run, Pallas kernels for 12% -> 15%
where the time goes in v3:
time: 117 us; the launch traced here: 116 us
  starting transfers between devices  51.1 us (44%)
  waiting for transfers between devices  38.3 us (33%)
  Pallas kernels  20.6 us (18%)
  local copies, waits for them, and re-layouts  3.86 us (3%)
  other arithmetic  1.46 us (1%)
    ppermute x28, starting transfers between devices, move(): return lax.ppermute(a, AXES, pairs(**offset))  41.6 us
    ppermute x28, waiting for transfers between devices, move(): return lax.ppermute(a, AXES, pairs(**offset))  28.1 us
    pallas_call x5, Pallas kernels, on_chip(): pl.pallas_call(kernel, in_specs=specs, out_specs=jax.tree.map(lambda _: p...  11.2 us
    all_to_all x1, waiting for transfers between devices, local(): lax.all_to_all(slotted, 'mod', split_axis=0, concat_axis=0, tiled=True)  10.1 us
    all_to_all x1, starting transfers between devices, local(): lax.all_to_all(slotted, 'mod', split_axis=0, concat_axis=0, tiled=True)  9.46 us
    pallas_call x2, Pallas kernels, columns_of(): pl.pallas_call(kernel, in_specs=[smem, pl.BlockSpec(memory_space=pl.ANY)]...  9.42 us
  transfers between devices with their start and end apart: 29, of which 16 were waited for; matrix products, arithmetic and copies ran while one was open for 1% of the time, Pallas kernels for 15%

profile of v3, /device:TPU:1, one launch (start us, length us, event | category | flops | bytes accessed | tf_op | source)
XLA Modules:
  0.0 116.5 jit_solution(6711731674710722863)
XLA Ops:
  3.2 9.5 %all-to-all-start = ((bf16[16,4,4096]{2,1,0:T(4,128)(2,1)}), bf16[16,4,4096]{2,1,0:T(4,128)(2,1)S(1)}, u32[]{:S(2)}, u32[]{:S(2)}) async-start(bf16[16,4,4096]{2,1,0:T(4,128)(2,1)} %copy.12), calls=%async_computation | async-start | bytes 1048576 | tf_op jit(solution)/shard_map/all_to_all | solution.py:158
  13.9 10.1 %all-to-all-done = bf16[16,4,4096]{2,1,0:T(4,128)(2,1)S(1)} async-done(((bf16[16,4,4096]{2,1,0:T(4,128)(2,1)}), bf16[16,4,4096]{2,1,0:T(4,128)(2,1)S(1)}, u32[]{:S(2)}, u32[]{:S(2)}) %all-to-all-start) | async-done | bytes 524320 | tf_op jit(solution)/shard_map/all_to_all | solution.py:158
  27.4 2.7 %collective-permute-start.6 = (bf16[32,4096]{1,0:T(8,128)(2,1)S(1)}, bf16[32,4096]{1,0:T(8,128)(2,1)S(1)}, u32[]{:S(2)}, u32[]{:S(2)}) collective-permute-start(bf16[32,4096]{1,0:T(8,128)(2,1)S(1)} %get-tuple-element.76.refs_0_), channel_id=1, source_target_pairs={{0,3},{1,0},{2,1},{3,2},{4,7},{5,4},{6,5},{7,6},{8,11},{9,8},{10,9... | collective-permute-start | bytes 786440 | tf_op jit(solution)/shard_map/ppermute | solution.py:28
  30.1 2.2 %collective-permute-done.refs_2_ = bf16[32,4096]{1,0:T(8,128)(2,1)S(1)} collective-permute-done((bf16[32,4096]{1,0:T(8,128)(2,1)S(1)}, bf16[32,4096]{1,0:T(8,128)(2,1)S(1)}, u32[]{:S(2)}, u32[]{:S(2)}) %collective-permute-start) | collective-permute-done | bytes 262176 | tf_op jit(solution)/shard_map/ppermute | solution.py:28
  32.3 2.4 %collective-permute-start.3 = (bf16[32,4096]{1,0:T(8,128)(2,1)S(1)}, bf16[32,4096]{1,0:T(8,128)(2,1)S(1)}, u32[]{:S(2)}, u32[]{:S(2)}) collective-permute-start(bf16[32,4096]{1,0:T(8,128)(2,1)S(1)} %collective-permute-done.1.refs_5_), channel_id=1, source_target_pairs={{0,3},{1,0},{2,1},{3,2},{4,7},{5,4},{6,5},{7,6},{8,11},{9,8},{10,9... | collective-permute-start | bytes 786440 | tf_op jit(solution)/shard_map/ppermute | solution.py:28
  34.7 3.2 %collective-permute-done.5.refs_3_ = bf16[32,4096]{1,0:T(8,128)(2,1)S(1)} collective-permute-done((bf16[32,4096]{1,0:T(8,128)(2,1)S(1)}, bf16[32,4096]{1,0:T(8,128)(2,1)S(1)}, u32[]{:S(2)}, u32[]{:S(2)}) %collective-permute-start.5) | collective-permute-done | bytes 262176 | tf_op jit(solution)/shard_map/ppermute | solution.py:28
  40.6 2.7 %collective-permute-done.3.refs_1_ = bf16[32,4096]{1,0:T(8,128)(2,1)S(1)} collective-permute-done((bf16[32,4096]{1,0:T(8,128)(2,1)S(1)}, bf16[32,4096]{1,0:T(8,128)(2,1)S(1)}, u32[]{:S(2)}, u32[]{:S(2)}) %collective-permute-start.3) | collective-permute-done | bytes 262176 | tf_op jit(solution)/shard_map/ppermute | solution.py:28
  44.7 5.0 %shard_map.56.refs_2_.refs_7_ = bf16[5,2048,512]{2,1,0:T(8,128)(2,1)S(1)} custom-call(s32[8]{0:T(128)S(1)} %stack.47.slots, bf16[2048,4096]{1,0:T(8,128)(2,1)} %bitcast.45), custom_call_target="tpu_custom_call" | custom-call | flops 1 | bytes 1 | tf_op jit(solution)/shard_map/pallas_call | solution.py:111
  52.3 2.2 %collective-permute-done.8.refs_3_ = bf16[64,4096]{1,0:T(8,128)(2,1)S(1)} collective-permute-done((bf16[64,4096]{1,0:T(8,128)(2,1)S(1)}, bf16[64,4096]{1,0:T(8,128)(2,1)S(1)}, u32[]{:S(2)}, u32[]{:S(2)}) %collective-permute-start.8) | collective-permute-done | bytes 524320 | tf_op jit(solution)/shard_map/ppermute | solution.py:28
  59.9 2.7 %collective-permute-start.13 = (bf16[256,512]{1,0:T(8,128)(2,1)S(1)}, bf16[256,512]{1,0:T(8,128)(2,1)S(1)}, u32[]{:S(2)}, u32[]{:S(2)}) collective-permute-start(bf16[256,512]{1,0:T(8,128)(2,1)S(1)} %get-tuple-element.54.refs_0_), channel_id=1, source_target_pairs={{0,3},{1,0},{2,1},{3,2},{4,7},{5,4},{6,5},{7,6},{8,11},{9,8},{10,9... | collective-permute-start | bytes 786440 | tf_op jit(solution)/shard_map/ppermute | solution.py:28
  62.5 4.4 %shard_map.58 = (f32[512,2048]{1,0:T(8,128)S(1)}, bf16[3,2048,512]{2,1,0:T(8,128)(2,1)S(1)}) custom-call(s32[8]{0:T(128)S(1)} %stack.47.slots, bf16[2048,4096]{1,0:T(8,128)(2,1)} %bitcast.46, bf16[256,512]{1,0:T(8,128)(2,1)S(1)} %get-tuple-element.54.refs_0_, bf16[256,512]{1,0:T(8,128)(2,1)S(1)} %get-tuple-element.53.refs_1_, ...), custom_call_target="tpu_custom_call" | custom-call | flops 1 | bytes 1 | tf_op jit(solution)/shard_map/pallas_call | solution.py:111
  67.1 2.7 %collective-permute-start.20 = (bf16[256,512]{1,0:T(8,128)(2,1)S(1)}, bf16[256,512]{1,0:T(8,128)(2,1)S(1)}, u32[]{:S(2)}, u32[]{:S(2)}) collective-permute-start(bf16[256,512]{1,0:T(8,128)(2,1)S(1)} %collective-permute-done.17.refs_3_), channel_id=1, source_target_pairs={{0,3},{1,0},{2,1},{3,2},{4,7},{5,4},{6,5},{7,6},{8,11},{9,8},{10,9... | collective-permute-start | bytes 786440 | tf_op jit(solution)/shard_map/ppermute | solution.py:28
  69.8 2.7 %collective-permute-start.15 = (bf16[512,512]{1,0:T(8,128)(2,1)S(1)}, bf16[512,512]{1,0:T(8,128)(2,1)S(1)}, u32[]{:S(2)}, u32[]{:S(2)}) collective-permute-start(bf16[512,512]{1,0:T(8,128)(2,1)S(1)} %collective-permute-done.11.refs_4_), channel_id=1, source_target_pairs={{0,3},{1,0},{2,1},{3,2},{4,7},{5,4},{6,5},{7,6},{8,11},{9,8},{10,9... | collective-permute-start | bytes 1572872 | tf_op jit(solution)/shard_map/ppermute | solution.py:28
  72.5 2.3 %collective-permute-done.18.refs_5_ = bf16[256,512]{1,0:T(8,128)(2,1)S(1)} collective-permute-done((bf16[256,512]{1,0:T(8,128)(2,1)S(1)}, bf16[256,512]{1,0:T(8,128)(2,1)S(1)}, u32[]{:S(2)}, u32[]{:S(2)}) %collective-permute-start.18) | collective-permute-done | bytes 262176 | tf_op jit(solution)/shard_map/ppermute | solution.py:28
  76.3 4.6 %shard_map.59.refs_4_ = f32[512,2048]{1,0:T(8,128)S(1)} custom-call(bf16[256,512]{1,0:T(8,128)(2,1)S(1)} %collective-permute-done.16.refs_0_, bf16[256,512]{1,0:T(8,128)(2,1)S(1)} %collective-permute-done.12.refs_1_, bf16[256,512]{1,0:T(8,128)(2,1)S(1)} %collective-permute-done.13.refs_2_, bf16[256,512]{1,0:T(8,128)(2,1)S(1)} %collective-permute-done.17.refs_3_, ...), custom_call_target="tpu_custom_call" | custom-call | flops 1 | bytes 1 | tf_op jit(solution)/shard_map/pallas_call | solution.py:50
  80.9 2.2 %collective-permute-done.21.refs_2_ = bf16[256,512]{1,0:T(8,128)(2,1)S(1)} collective-permute-done((bf16[256,512]{1,0:T(8,128)(2,1)S(1)}, bf16[256,512]{1,0:T(8,128)(2,1)S(1)}, u32[]{:S(2)}, u32[]{:S(2)}) %collective-permute-start.21) | collective-permute-done | bytes 262176 | tf_op jit(solution)/shard_map/ppermute | solution.py:28
  83.2 2.2 %collective-permute-done.14.refs_0_ = bf16[512,512]{1,0:T(8,128)(2,1)S(1)} collective-permute-done((bf16[512,512]{1,0:T(8,128)(2,1)S(1)}, bf16[512,512]{1,0:T(8,128)(2,1)S(1)}, u32[]{:S(2)}, u32[]{:S(2)}) %collective-permute-start.14) | collective-permute-done | bytes 524320 | tf_op jit(solution)/shard_map/ppermute | solution.py:28
  88.2 5.1 %collective-permute-start.22 = (bf16[256,2048]{1,0:T(8,128)(2,1)S(1)}, bf16[256,2048]{1,0:T(8,128)(2,1)S(1)}, u32[]{:S(2)}, u32[]{:S(2)}) collective-permute-start(bf16[256,2048]{1,0:T(8,128)(2,1)S(1)} %shard_map.61), channel_id=1, source_target_pairs={{0,8},{1,9},{2,10},{3,11},{4,12},{5,13},{6,14},{7,15},{8,0},{9,1},... | collective-permute-start | bytes 3145736 | tf_op jit(solution)/shard_map/ppermute | solution.py:28
  96.1 3.9 %collective-permute-start.23 = (bf16[64,2048]{1,0:T(8,128)(2,1)S(1)}, bf16[64,2048]{1,0:T(8,128)(2,1)S(1)}, u32[]{:S(2)}, u32[]{:S(2)}) collective-permute-start(bf16[64,2048]{1,0:T(8,128)(2,1)S(1)} %get-tuple-element.71), channel_id=1, source_target_pairs={{8,24},{9,25},{10,26},{11,27},{12,28},{13,29},{14,30},{15,31},{24,... | collective-permute-start | bytes 786440 | tf_op jit(solution)/shard_map/ppermute | solution.py:28
  101.2 2.7 %collective-permute-start.25 = (bf16[64,2048]{1,0:T(8,128)(2,1)S(1)}, bf16[64,2048]{1,0:T(8,128)(2,1)S(1)}, u32[]{:S(2)}, u32[]{:S(2)}) collective-permute-start(bf16[64,2048]{1,0:T(8,128)(2,1)S(1)} %get-tuple-element.73), channel_id=1, source_target_pairs={{0,64},{1,65},{2,66},{3,67},{4,68},{5,69},{6,70},{7,71},{8,88},{9,... | collective-permute-start | bytes 786440 | tf_op jit(solution)/shard_map/ppermute | solution.py:28
  104.0 2.7 %collective-permute-start.26 = (bf16[64,2048]{1,0:T(8,128)(2,1)S(1)}, bf16[64,2048]{1,0:T(8,128)(2,1)S(1)}, u32[]{:S(2)}, u32[]{:S(2)}) collective-permute-start(bf16[64,2048]{1,0:T(8,128)(2,1)S(1)} %get-tuple-element.72), channel_id=1, source_target_pairs={{0,96},{1,97},{2,98},{3,99},{4,100},{5,101},{6,102},{7,103},{8,120... | collective-permute-start | bytes 786440 | tf_op jit(solution)/shard_map/ppermute | solution.py:28
  106.6 2.6 %collective-permute-done.24 = bf16[64,2048]{1,0:T(8,128)(2,1)S(1)} collective-permute-done((bf16[64,2048]{1,0:T(8,128)(2,1)S(1)}, bf16[64,2048]{1,0:T(8,128)(2,1)S(1)}, u32[]{:S(2)}, u32[]{:S(2)}) %collective-permute-start.24) | collective-permute-done | bytes 262176 | tf_op jit(solution)/shard_map/ppermute | solution.py:28
  109.2 2.6 %collective-permute-done.25 = bf16[64,2048]{1,0:T(8,128)(2,1)S(1)} collective-permute-done((bf16[64,2048]{1,0:T(8,128)(2,1)S(1)}, bf16[64,2048]{1,0:T(8,128)(2,1)S(1)}, u32[]{:S(2)}, u32[]{:S(2)}) %collective-permute-start.25) | collective-permute-done | bytes 262176 | tf_op jit(solution)/shard_map/ppermute | solution.py:28
  111.8 2.1 %collective-permute-done.26 = bf16[64,2048]{1,0:T(8,128)(2,1)S(1)} collective-permute-done((bf16[64,2048]{1,0:T(8,128)(2,1)S(1)}, bf16[64,2048]{1,0:T(8,128)(2,1)S(1)}, u32[]{:S(2)}, u32[]{:S(2)}) %collective-permute-start.26) | collective-permute-done | bytes 262176 | tf_op jit(solution)/shard_map/ppermute | solution.py:28
  (69 shorter events, 30.8 us)
Async XLA Ops:
  3.2 20.8 %all-to-all-start = ((bf16[16,4,4096]{2,1,0:T(4,128)(2,1)}), bf16[16,4,4096]{2,1,0:T(4,128)(2,1)S(1)}, u32[]{:S(2)}, u32[]{:S(2)}) async-start(bf16[16,4,4096]{2,1,0:T(4,128)(2,1)} %copy.12), calls=%async_computation | async-start | bytes 1048576 | tf_op jit(solution)/shard_map/all_to_all | solution.py:158
  24.1 13.8 %collective-permute-start.4 = (bf16[64,4096]{1,0:T(8,128)(2,1)S(1)}, bf16[64,4096]{1,0:T(8,128)(2,1)S(1)}, u32[]{:S(2)}, u32[]{:S(2)}) collective-permute-start(bf16[64,4096]{1,0:T(8,128)(2,1)S(1)} %reshape.441), channel_id=1, source_target_pairs={{0,4},{1,5},{2,6},{3,7},{4,0},{5,1},{6,2},{7,3},{8,12},{9,13},{10,... | collective-permute-start | bytes 1572872 | tf_op jit(solution)/shard_map/ppermute | solution.py:28
  24.7 7.6 %collective-permute-start = (bf16[32,4096]{1,0:T(8,128)(2,1)S(1)}, bf16[32,4096]{1,0:T(8,128)(2,1)S(1)}, u32[]{:S(2)}, u32[]{:S(2)}) collective-permute-start(bf16[32,4096]{1,0:T(8,128)(2,1)S(1)} %get-tuple-element.76.refs_0_), channel_id=1, source_target_pairs={{0,1},{1,2},{2,3},{3,0},{4,5},{5,6},{6,7},{7,4},{8,9},{9,10},{10,1... | collective-permute-start | bytes 786440 | tf_op jit(solution)/shard_map/ppermute | solution.py:28
  27.4 10.5 %collective-permute-start.5 = (bf16[32,4096]{1,0:T(8,128)(2,1)S(1)}, bf16[32,4096]{1,0:T(8,128)(2,1)S(1)}, u32[]{:S(2)}, u32[]{:S(2)}) collective-permute-start(bf16[32,4096]{1,0:T(8,128)(2,1)S(1)} %get-tuple-element.75.refs_1_), channel_id=1, source_target_pairs={{0,1},{1,2},{2,3},{3,0},{4,5},{5,6},{6,7},{7,4},{8,9},{9,10},{10,1... | collective-permute-start | bytes 786440 | tf_op jit(solution)/shard_map/ppermute | solution.py:28
  27.4 10.5 %collective-permute-start.6 = (bf16[32,4096]{1,0:T(8,128)(2,1)S(1)}, bf16[32,4096]{1,0:T(8,128)(2,1)S(1)}, u32[]{:S(2)}, u32[]{:S(2)}) collective-permute-start(bf16[32,4096]{1,0:T(8,128)(2,1)S(1)} %get-tuple-element.76.refs_0_), channel_id=1, source_target_pairs={{0,3},{1,0},{2,1},{3,2},{4,7},{5,4},{6,5},{7,6},{8,11},{9,8},{10,9... | collective-permute-start | bytes 786440 | tf_op jit(solution)/shard_map/ppermute | solution.py:28
  32.3 11.0 %collective-permute-start.3 = (bf16[32,4096]{1,0:T(8,128)(2,1)S(1)}, bf16[32,4096]{1,0:T(8,128)(2,1)S(1)}, u32[]{:S(2)}, u32[]{:S(2)}) collective-permute-start(bf16[32,4096]{1,0:T(8,128)(2,1)S(1)} %collective-permute-done.1.refs_5_), channel_id=1, source_target_pairs={{0,3},{1,0},{2,1},{3,2},{4,7},{5,4},{6,5},{7,6},{8,11},{9,8},{10,9... | collective-permute-start | bytes 786440 | tf_op jit(solution)/shard_map/ppermute | solution.py:28
  34.7 9.6 %collective-permute-start.2 = (bf16[32,4096]{1,0:T(8,128)(2,1)S(1)}, bf16[32,4096]{1,0:T(8,128)(2,1)S(1)}, u32[]{:S(2)}, u32[]{:S(2)}) collective-permute-start(bf16[32,4096]{1,0:T(8,128)(2,1)S(1)} %collective-permute-done.refs_2_), channel_id=1, source_target_pairs={{0,1},{1,2},{2,3},{3,0},{4,5},{5,6},{6,7},{7,4},{8,9},{9,10},{10,1... | collective-permute-start | bytes 786440 | tf_op jit(solution)/shard_map/ppermute | solution.py:28
  37.9 14.4 %collective-permute-start.7 = (bf16[64,4096]{1,0:T(8,128)(2,1)S(1)}, bf16[64,4096]{1,0:T(8,128)(2,1)S(1)}, u32[]{:S(2)}, u32[]{:S(2)}) collective-permute-start(bf16[64,4096]{1,0:T(8,128)(2,1)S(1)} %collective-permute-done.4.refs_6_), channel_id=1, source_target_pairs={{0,1},{1,2},{2,3},{3,0},{4,5},{5,6},{6,7},{7,4},{8,9},{9,10},{10,1... | collective-permute-start | bytes 1572872 | tf_op jit(solution)/shard_map/ppermute | solution.py:28
  38.8 15.6 %collective-permute-start.8 = (bf16[64,4096]{1,0:T(8,128)(2,1)S(1)}, bf16[64,4096]{1,0:T(8,128)(2,1)S(1)}, u32[]{:S(2)}, u32[]{:S(2)}) collective-permute-start(bf16[64,4096]{1,0:T(8,128)(2,1)S(1)} %collective-permute-done.4.refs_6_), channel_id=1, source_target_pairs={{0,3},{1,0},{2,1},{3,2},{4,7},{5,4},{6,5},{7,6},{8,11},{9,8},{10,9... | collective-permute-start | bytes 1572872 | tf_op jit(solution)/shard_map/ppermute | solution.py:28
  43.2 8.1 %collective-permute-start.10 = (bf16[32,4096]{1,0:T(8,128)(2,1)S(1)}, bf16[32,4096]{1,0:T(8,128)(2,1)S(1)}, u32[]{:S(2)}, u32[]{:S(2)}) collective-permute-start(bf16[32,4096]{1,0:T(8,128)(2,1)S(1)} %collective-permute-done.3.refs_1_), channel_id=1, source_target_pairs={{0,4},{1,5},{2,6},{3,7},{4,0},{5,1},{6,2},{7,3},{8,12},{9,13},{10,... | collective-permute-start | bytes 786440 | tf_op jit(solution)/shard_map/ppermute | solution.py:28
  56.0 13.7 %collective-permute-start.11 = (bf16[512,512]{1,0:T(8,128)(2,1)S(1)}, bf16[512,512]{1,0:T(8,128)(2,1)S(1)}, u32[]{:S(2)}, u32[]{:S(2)}) collective-permute-start(bf16[512,512]{1,0:T(8,128)(2,1)S(1)} %get-tuple-element.52), channel_id=1, source_target_pairs={{0,4},{1,5},{2,6},{3,7},{4,0},{5,1},{6,2},{7,3},{8,12},{9,13},{10,... | collective-permute-start | bytes 1572872 | tf_op jit(solution)/shard_map/ppermute | solution.py:28
  57.2 9.8 %collective-permute-start.16 = (bf16[256,512]{1,0:T(8,128)(2,1)S(1)}, bf16[256,512]{1,0:T(8,128)(2,1)S(1)}, u32[]{:S(2)}, u32[]{:S(2)}) collective-permute-start(bf16[256,512]{1,0:T(8,128)(2,1)S(1)} %get-tuple-element.54.refs_0_), channel_id=1, source_target_pairs={{0,1},{1,2},{2,3},{3,0},{4,5},{5,6},{6,7},{7,4},{8,9},{9,10},{10,1... | collective-permute-start | bytes 786440 | tf_op jit(solution)/shard_map/ppermute | solution.py:28
  58.4 8.6 %collective-permute-start.17 = (bf16[256,512]{1,0:T(8,128)(2,1)S(1)}, bf16[256,512]{1,0:T(8,128)(2,1)S(1)}, u32[]{:S(2)}, u32[]{:S(2)}) collective-permute-start(bf16[256,512]{1,0:T(8,128)(2,1)S(1)} %get-tuple-element.53.refs_1_), channel_id=1, source_target_pairs={{0,3},{1,0},{2,1},{3,2},{4,7},{5,4},{6,5},{7,6},{8,11},{9,8},{10,9... | collective-permute-start | bytes 786440 | tf_op jit(solution)/shard_map/ppermute | solution.py:28
  59.9 9.9 %collective-permute-start.12 = (bf16[256,512]{1,0:T(8,128)(2,1)S(1)}, bf16[256,512]{1,0:T(8,128)(2,1)S(1)}, u32[]{:S(2)}, u32[]{:S(2)}) collective-permute-start(bf16[256,512]{1,0:T(8,128)(2,1)S(1)} %get-tuple-element.53.refs_1_), channel_id=1, source_target_pairs={{0,1},{1,2},{2,3},{3,0},{4,5},{5,6},{6,7},{7,4},{8,9},{9,10},{10,1... | collective-permute-start | bytes 786440 | tf_op jit(solution)/shard_map/ppermute | solution.py:28
  59.9 9.9 %collective-permute-start.13 = (bf16[256,512]{1,0:T(8,128)(2,1)S(1)}, bf16[256,512]{1,0:T(8,128)(2,1)S(1)}, u32[]{:S(2)}, u32[]{:S(2)}) collective-permute-start(bf16[256,512]{1,0:T(8,128)(2,1)S(1)} %get-tuple-element.54.refs_0_), channel_id=1, source_target_pairs={{0,3},{1,0},{2,1},{3,2},{4,7},{5,4},{6,5},{7,6},{8,11},{9,8},{10,9... | collective-permute-start | bytes 786440 | tf_op jit(solution)/shard_map/ppermute | solution.py:28
  67.0 7.8 %collective-permute-start.18 = (bf16[256,512]{1,0:T(8,128)(2,1)S(1)}, bf16[256,512]{1,0:T(8,128)(2,1)S(1)}, u32[]{:S(2)}, u32[]{:S(2)}) collective-permute-start(bf16[256,512]{1,0:T(8,128)(2,1)S(1)} %collective-permute-done.16.refs_0_), channel_id=1, source_target_pairs={{0,1},{1,2},{2,3},{3,0},{4,5},{5,6},{6,7},{7,4},{8,9},{9,10},{10,1... | collective-permute-start | bytes 786440 | tf_op jit(solution)/shard_map/ppermute | solution.py:28
  67.1 8.2 %collective-permute-start.20 = (bf16[256,512]{1,0:T(8,128)(2,1)S(1)}, bf16[256,512]{1,0:T(8,128)(2,1)S(1)}, u32[]{:S(2)}, u32[]{:S(2)}) collective-permute-start(bf16[256,512]{1,0:T(8,128)(2,1)S(1)} %collective-permute-done.17.refs_3_), channel_id=1, source_target_pairs={{0,3},{1,0},{2,1},{3,2},{4,7},{5,4},{6,5},{7,6},{8,11},{9,8},{10,9... | collective-permute-start | bytes 786440 | tf_op jit(solution)/shard_map/ppermute | solution.py:28
  69.8 15.7 %collective-permute-start.14 = (bf16[512,512]{1,0:T(8,128)(2,1)S(1)}, bf16[512,512]{1,0:T(8,128)(2,1)S(1)}, u32[]{:S(2)}, u32[]{:S(2)}) collective-permute-start(bf16[512,512]{1,0:T(8,128)(2,1)S(1)} %collective-permute-done.11.refs_4_), channel_id=1, source_target_pairs={{0,1},{1,2},{2,3},{3,0},{4,5},{5,6},{6,7},{7,4},{8,9},{9,10},{10,1... | collective-permute-start | bytes 1572872 | tf_op jit(solution)/shard_map/ppermute | solution.py:28
  69.8 16.4 %collective-permute-start.15 = (bf16[512,512]{1,0:T(8,128)(2,1)S(1)}, bf16[512,512]{1,0:T(8,128)(2,1)S(1)}, u32[]{:S(2)}, u32[]{:S(2)}) collective-permute-start(bf16[512,512]{1,0:T(8,128)(2,1)S(1)} %collective-permute-done.11.refs_4_), channel_id=1, source_target_pairs={{0,3},{1,0},{2,1},{3,2},{4,7},{5,4},{6,5},{7,6},{8,11},{9,8},{10,9... | collective-permute-start | bytes 1572872 | tf_op jit(solution)/shard_map/ppermute | solution.py:28
  75.3 7.9 %collective-permute-start.21 = (bf16[256,512]{1,0:T(8,128)(2,1)S(1)}, bf16[256,512]{1,0:T(8,128)(2,1)S(1)}, u32[]{:S(2)}, u32[]{:S(2)}) collective-permute-start(bf16[256,512]{1,0:T(8,128)(2,1)S(1)} %collective-permute-done.20.refs_6_), channel_id=1, source_target_pairs={{0,4},{1,5},{2,6},{3,7},{4,0},{5,1},{6,2},{7,3},{8,12},{9,13},{10,... | collective-permute-start | bytes 786440 | tf_op jit(solution)/shard_map/ppermute | solution.py:28
  96.1 10.6 %collective-permute-start.23 = (bf16[64,2048]{1,0:T(8,128)(2,1)S(1)}, bf16[64,2048]{1,0:T(8,128)(2,1)S(1)}, u32[]{:S(2)}, u32[]{:S(2)}) collective-permute-start(bf16[64,2048]{1,0:T(8,128)(2,1)S(1)} %get-tuple-element.71), channel_id=1, source_target_pairs={{8,24},{9,25},{10,26},{11,27},{12,28},{13,29},{14,30},{15,31},{24,... | collective-permute-start | bytes 786440 | tf_op jit(solution)/shard_map/ppermute | solution.py:28
  100.0 9.2 %collective-permute-start.24 = (bf16[64,2048]{1,0:T(8,128)(2,1)S(1)}, bf16[64,2048]{1,0:T(8,128)(2,1)S(1)}, u32[]{:S(2)}, u32[]{:S(2)}) collective-permute-start(bf16[64,2048]{1,0:T(8,128)(2,1)S(1)} %get-tuple-element.74), channel_id=1, source_target_pairs={{0,32},{1,33},{2,34},{3,35},{4,36},{5,37},{6,38},{7,39},{8,56},{9,... | collective-permute-start | bytes 786440 | tf_op jit(solution)/shard_map/ppermute | solution.py:28
  101.2 10.5 %collective-permute-start.25 = (bf16[64,2048]{1,0:T(8,128)(2,1)S(1)}, bf16[64,2048]{1,0:T(8,128)(2,1)S(1)}, u32[]{:S(2)}, u32[]{:S(2)}) collective-permute-start(bf16[64,2048]{1,0:T(8,128)(2,1)S(1)} %get-tuple-element.73), channel_id=1, source_target_pairs={{0,64},{1,65},{2,66},{3,67},{4,68},{5,69},{6,70},{7,71},{8,88},{9,... | collective-permute-start | bytes 786440 | tf_op jit(solution)/shard_map/ppermute | solution.py:28
  104.0 9.9 %collective-permute-start.26 = (bf16[64,2048]{1,0:T(8,128)(2,1)S(1)}, bf16[64,2048]{1,0:T(8,128)(2,1)S(1)}, u32[]{:S(2)}, u32[]{:S(2)}) collective-permute-start(bf16[64,2048]{1,0:T(8,128)(2,1)S(1)} %get-tuple-element.72), channel_id=1, source_target_pairs={{0,96},{1,97},{2,98},{3,99},{4,100},{5,101},{6,102},{7,103},{8,120... | collective-permute-start | bytes 786440 | tf_op jit(solution)/shard_map/ppermute | solution.py:28
  (8 other events, 56.2 us)

commit v4 on v3

--- a/solution.py
+++ b/solution.py
@@ -19,7 +19,7 @@
             core = mod % 2
             dyh = yh[core] if isinstance(yh, tuple) else yh
             to_mod = ((mod // 4 + z) % 4) * 4 + ((mod // 2 % 2) ^ dyh) * 2 + (core ^ c)
-            to_ex = ((ex // 4) ^ yl) * 4 + (ex % 4 + x) % 4
+            to_ex = ((ex // 4) ^ yl) * 4 + (ex % 4 + (x if core == 0 else -x)) % 4
             out.append((mod * 8 + ex, to_mod * 8 + to_ex))
     return out
 
@@ -163,14 +163,15 @@
     row = jnp.stack([jnp.where(c == 0, yhs[s], yhs[s][:, ::-1]) for s in (0, 1)])
     row = jnp.stack([row[0], row[1][:, ::-1]]).reshape(1, 512)
     source = row // 4 % 8
-    dx, dy = (source % 4 - x) % 4, (source // 4) ^ yl
+    way = 1 - 2 * c
+    dx, dy = (source % 4 - x) * way % 4, (source // 4) ^ yl
     block = jnp.where(
         dy == 0,
         jnp.where(dx == 0, 0, jnp.where(dx == 3, 1, jnp.where(dx == 1, 2, 4))),
         jnp.where(dx == 0, 3, jnp.where(dx == 3, 5, jnp.where(dx == 1, 6, 7))),
     )
     place = block * 64 + (row // 32) * 4 + row % 4
-    left, right, over = (x + 3) % 4, (x + 1) % 4, (x + 2) % 4
+    left, right, over = (x - way) % 4, (x + way) % 4, (x + 2) % 4
     here, there = yl * 4, (1 - yl) * 4
     slots = [here + x, here + left, here + right, there + x, here + over, there + left, there + right, there + over]
     own, place, slots = lax.optimization_barrier((own, place, jnp.stack(slots).astype(jnp.int32)))

time: 117 us -> 120 us (1.026)
  waiting for transfers between devices: 38.3 us -> 49.1 us
  starting transfers between devices: 51.1 us -> 43.4 us
    ppermute x28, waiting for transfers between devices: 28.1 us -> 39 us  [move(): return lax.ppermute(a, AXES, pairs(**offset))]
    ppermute x28, starting transfers between devices: 41.6 us -> 33.9 us  [move(): return lax.ppermute(a, AXES, pairs(**offset))]
  transfers between devices with their start and end apart: 29 -> 29, of which waited for: 16 -> 16; matrix products, arithmetic and copies ran while one was open for 1% -> 1% of each run, Pallas kernels for 15% -> 14%
where the time goes in v4:
time: 120 us
  waiting for transfers between devices  49.1 us (41%)
  starting transfers between devices  43.4 us (36%)
  Pallas kernels  20.6 us (17%)
  local copies, waits for them, and re-layouts  3.86 us (3%)
  other arithmetic  1.46 us (1%)
    ppermute x28, waiting for transfers between devices, move(): return lax.ppermute(a, AXES, pairs(**offset))  39 us
    ppermute x28, starting transfers between devices, move(): return lax.ppermute(a, AXES, pairs(**offset))  33.9 us
    pallas_call x5, Pallas kernels, on_chip(): pl.pallas_call(kernel, in_specs=specs, out_specs=jax.tree.map(lambda _: p...  11.2 us
    all_to_all x1, waiting for transfers between devices, local(): lax.all_to_all(slotted, 'mod', split_axis=0, concat_axis=0, tiled=True)  10.1 us
    all_to_all x1, starting transfers between devices, local(): lax.all_to_all(slotted, 'mod', split_axis=0, concat_axis=0, tiled=True)  9.46 us
    pallas_call x2, Pallas kernels, columns_of(): pl.pallas_call(kernel, in_specs=[smem, pl.BlockSpec(memory_space=pl.ANY)]...  9.42 us
  transfers between devices with their start and end apart: 29, of which 16 were waited for; matrix products, arithmetic and copies ran while one was open for 1% of the time, Pallas kernels for 14%

profile of v4, /device:TPU:1, one launch (start us, length us, event | category | flops | bytes accessed | tf_op | source)
XLA Modules:
  0.0 119.6 jit_solution(14221055070857334987)
XLA Ops:
  3.2 9.5 %all-to-all-start = ((bf16[16,4,4096]{2,1,0:T(4,128)(2,1)}), bf16[16,4,4096]{2,1,0:T(4,128)(2,1)S(1)}, u32[]{:S(2)}, u32[]{:S(2)}) async-start(bf16[16,4,4096]{2,1,0:T(4,128)(2,1)} %copy.12), calls=%async_computation | async-start | bytes 1048576 | tf_op jit(solution)/shard_map/all_to_all | solution.py:158
  13.9 10.1 %all-to-all-done = bf16[16,4,4096]{2,1,0:T(4,128)(2,1)S(1)} async-done(((bf16[16,4,4096]{2,1,0:T(4,128)(2,1)}), bf16[16,4,4096]{2,1,0:T(4,128)(2,1)S(1)}, u32[]{:S(2)}, u32[]{:S(2)}) %all-to-all-start) | async-done | bytes 524320 | tf_op jit(solution)/shard_map/all_to_all | solution.py:158
  24.7 2.5 %collective-permute-start = (bf16[32,4096]{1,0:T(8,128)(2,1)S(1)}, bf16[32,4096]{1,0:T(8,128)(2,1)S(1)}, u32[]{:S(2)}, u32[]{:S(2)}) collective-permute-start(bf16[32,4096]{1,0:T(8,128)(2,1)S(1)} %get-tuple-element.76.refs_0_), channel_id=1, source_target_pairs={{0,1},{1,2},{2,3},{3,0},{4,5},{5,6},{6,7},{7,4},{8,11},{9,8},{10,9... | collective-permute-start | bytes 786440 | tf_op jit(solution)/shard_map/ppermute | solution.py:28
  27.2 2.7 %collective-permute-start.5 = (bf16[32,4096]{1,0:T(8,128)(2,1)S(1)}, bf16[32,4096]{1,0:T(8,128)(2,1)S(1)}, u32[]{:S(2)}, u32[]{:S(2)}) collective-permute-start(bf16[32,4096]{1,0:T(8,128)(2,1)S(1)} %get-tuple-element.75.refs_1_), channel_id=1, source_target_pairs={{0,1},{1,2},{2,3},{3,0},{4,5},{5,6},{6,7},{7,4},{8,11},{9,8},{10,9... | collective-permute-start | bytes 786440 | tf_op jit(solution)/shard_map/ppermute | solution.py:28
  30.9 5.8 %collective-permute-done.1.refs_5_ = bf16[32,4096]{1,0:T(8,128)(2,1)S(1)} collective-permute-done((bf16[32,4096]{1,0:T(8,128)(2,1)S(1)}, bf16[32,4096]{1,0:T(8,128)(2,1)S(1)}, u32[]{:S(2)}, u32[]{:S(2)}) %collective-permute-start.1) | collective-permute-done | bytes 262176 | tf_op jit(solution)/shard_map/ppermute | solution.py:28
  36.7 2.7 %collective-permute-start.2 = (bf16[32,4096]{1,0:T(8,128)(2,1)S(1)}, bf16[32,4096]{1,0:T(8,128)(2,1)S(1)}, u32[]{:S(2)}, u32[]{:S(2)}) collective-permute-start(bf16[32,4096]{1,0:T(8,128)(2,1)S(1)} %collective-permute-done.refs_2_), channel_id=1, source_target_pairs={{0,1},{1,2},{2,3},{3,0},{4,5},{5,6},{6,7},{7,4},{8,11},{9,8},{10,9... | collective-permute-start | bytes 786440 | tf_op jit(solution)/shard_map/ppermute | solution.py:28
  39.4 2.1 %collective-permute-done.6.refs_4_ = bf16[32,4096]{1,0:T(8,128)(2,1)S(1)} collective-permute-done((bf16[32,4096]{1,0:T(8,128)(2,1)S(1)}, bf16[32,4096]{1,0:T(8,128)(2,1)S(1)}, u32[]{:S(2)}, u32[]{:S(2)}) %collective-permute-start.6) | collective-permute-done | bytes 262176 | tf_op jit(solution)/shard_map/ppermute | solution.py:28
  43.0 1.9 %collective-permute-done.3.refs_1_ = bf16[32,4096]{1,0:T(8,128)(2,1)S(1)} collective-permute-done((bf16[32,4096]{1,0:T(8,128)(2,1)S(1)}, bf16[32,4096]{1,0:T(8,128)(2,1)S(1)}, u32[]{:S(2)}, u32[]{:S(2)}) %collective-permute-start.3) | collective-permute-done | bytes 262176 | tf_op jit(solution)/shard_map/ppermute | solution.py:28
  46.4 5.0 %shard_map.56.refs_2_.refs_7_ = bf16[5,2048,512]{2,1,0:T(8,128)(2,1)S(1)} custom-call(s32[8]{0:T(128)S(1)} %stack.47.slots, bf16[2048,4096]{1,0:T(8,128)(2,1)} %bitcast.45), custom_call_target="tpu_custom_call" | custom-call | flops 1 | bytes 1 | tf_op jit(solution)/shard_map/pallas_call | solution.py:111
  53.0 3.7 %collective-permute-done.9.refs_4_ = bf16[32,4096]{1,0:T(8,128)(2,1)S(1)} collective-permute-done((bf16[32,4096]{1,0:T(8,128)(2,1)S(1)}, bf16[32,4096]{1,0:T(8,128)(2,1)S(1)}, u32[]{:S(2)}, u32[]{:S(2)}) %collective-permute-start.9) | collective-permute-done | bytes 262176 | tf_op jit(solution)/shard_map/ppermute | solution.py:28
  59.4 2.8 %collective-permute-start.16 = (bf16[256,512]{1,0:T(8,128)(2,1)S(1)}, bf16[256,512]{1,0:T(8,128)(2,1)S(1)}, u32[]{:S(2)}, u32[]{:S(2)}) collective-permute-start(bf16[256,512]{1,0:T(8,128)(2,1)S(1)} %get-tuple-element.54.refs_0_), channel_id=1, source_target_pairs={{0,1},{1,2},{2,3},{3,0},{4,5},{5,6},{6,7},{7,4},{8,11},{9,8},{10,9... | collective-permute-start | bytes 786440 | tf_op jit(solution)/shard_map/ppermute | solution.py:28
  62.2 2.7 %collective-permute-start.12 = (bf16[256,512]{1,0:T(8,128)(2,1)S(1)}, bf16[256,512]{1,0:T(8,128)(2,1)S(1)}, u32[]{:S(2)}, u32[]{:S(2)}) collective-permute-start(bf16[256,512]{1,0:T(8,128)(2,1)S(1)} %get-tuple-element.53.refs_1_), channel_id=1, source_target_pairs={{0,1},{1,2},{2,3},{3,0},{4,5},{5,6},{6,7},{7,4},{8,11},{9,8},{10,9... | collective-permute-start | bytes 786440 | tf_op jit(solution)/shard_map/ppermute | solution.py:28
  64.9 4.4 %shard_map.58 = (f32[512,2048]{1,0:T(8,128)S(1)}, bf16[3,2048,512]{2,1,0:T(8,128)(2,1)S(1)}) custom-call(s32[8]{0:T(128)S(1)} %stack.47.slots, bf16[2048,4096]{1,0:T(8,128)(2,1)} %bitcast.46, bf16[256,512]{1,0:T(8,128)(2,1)S(1)} %get-tuple-element.54.refs_0_, bf16[256,512]{1,0:T(8,128)(2,1)S(1)} %get-tuple-element.53.refs_1_, ...), custom_call_target="tpu_custom_call" | custom-call | flops 1 | bytes 1 | tf_op jit(solution)/shard_map/pallas_call | solution.py:111
  69.3 2.0 %collective-permute-done.17.refs_3_ = bf16[256,512]{1,0:T(8,128)(2,1)S(1)} collective-permute-done((bf16[256,512]{1,0:T(8,128)(2,1)S(1)}, bf16[256,512]{1,0:T(8,128)(2,1)S(1)}, u32[]{:S(2)}, u32[]{:S(2)}) %collective-permute-start.17) | collective-permute-done | bytes 262176 | tf_op jit(solution)/shard_map/ppermute | solution.py:28
  72.8 4.1 %collective-permute-done.13.refs_2_ = bf16[256,512]{1,0:T(8,128)(2,1)S(1)} collective-permute-done((bf16[256,512]{1,0:T(8,128)(2,1)S(1)}, bf16[256,512]{1,0:T(8,128)(2,1)S(1)}, u32[]{:S(2)}, u32[]{:S(2)}) %collective-permute-start.13) | collective-permute-done | bytes 262176 | tf_op jit(solution)/shard_map/ppermute | solution.py:28
  78.8 3.7 %collective-permute-done.20.refs_6_ = bf16[256,512]{1,0:T(8,128)(2,1)S(1)} collective-permute-done((bf16[256,512]{1,0:T(8,128)(2,1)S(1)}, bf16[256,512]{1,0:T(8,128)(2,1)S(1)}, u32[]{:S(2)}, u32[]{:S(2)}) %collective-permute-start.20) | collective-permute-done | bytes 262176 | tf_op jit(solution)/shard_map/ppermute | solution.py:28
  83.0 4.6 %shard_map.59.refs_4_ = f32[512,2048]{1,0:T(8,128)S(1)} custom-call(bf16[256,512]{1,0:T(8,128)(2,1)S(1)} %collective-permute-done.16.refs_0_, bf16[256,512]{1,0:T(8,128)(2,1)S(1)} %collective-permute-done.12.refs_1_, bf16[256,512]{1,0:T(8,128)(2,1)S(1)} %collective-permute-done.13.refs_2_, bf16[256,512]{1,0:T(8,128)(2,1)S(1)} %collective-permute-done.17.refs_3_, ...), custom_call_target="tpu_custom_call" | custom-call | flops 1 | bytes 1 | tf_op jit(solution)/shard_map/pallas_call | solution.py:50
  89.1 4.6 %collective-permute-done.15.refs_1_ = bf16[512,512]{1,0:T(8,128)(2,1)S(1)} collective-permute-done((bf16[512,512]{1,0:T(8,128)(2,1)S(1)}, bf16[512,512]{1,0:T(8,128)(2,1)S(1)}, u32[]{:S(2)}, u32[]{:S(2)}) %collective-permute-start.15) | collective-permute-done | bytes 524320 | tf_op jit(solution)/shard_map/ppermute | solution.py:28
  96.5 1.9 %shard_map.60 = f32[256,2048]{1,0:T(8,128)S(1)} custom-call(bf16[512,512]{1,0:T(8,128)(2,1)S(1)} %collective-permute-done.14.refs_0_, bf16[512,512]{1,0:T(8,128)(2,1)S(1)} %collective-permute-done.15.refs_1_, bf16[256,512]{1,0:T(8,128)(2,1)S(1)} %collective-permute-done.21.refs_2_, bf16[3,2048,512]{2,1,0:T(8,128)(2,1)S(1)} %get-tuple-element.64.refs_3_, ...), custom_call_target="tpu_custom_call" | custom-call | flops 1 | bytes 1 | tf_op jit(solution)/shard_map/pallas_call | solution.py:50
  99.4 3.0 %collective-permute-start.23 = (bf16[64,2048]{1,0:T(8,128)(2,1)S(1)}, bf16[64,2048]{1,0:T(8,128)(2,1)S(1)}, u32[]{:S(2)}, u32[]{:S(2)}) collective-permute-start(bf16[64,2048]{1,0:T(8,128)(2,1)S(1)} %get-tuple-element.71), channel_id=1, source_target_pairs={{8,24},{9,25},{10,26},{11,27},{12,28},{13,29},{14,30},{15,31},{24,... | collective-permute-start | bytes 786440 | tf_op jit(solution)/shard_map/ppermute | solution.py:28
  103.7 2.4 %collective-permute-start.25 = (bf16[64,2048]{1,0:T(8,128)(2,1)S(1)}, bf16[64,2048]{1,0:T(8,128)(2,1)S(1)}, u32[]{:S(2)}, u32[]{:S(2)}) collective-permute-start(bf16[64,2048]{1,0:T(8,128)(2,1)S(1)} %get-tuple-element.73), channel_id=1, source_target_pairs={{0,64},{1,65},{2,66},{3,67},{4,68},{5,69},{6,70},{7,71},{8,88},{9,... | collective-permute-start | bytes 786440 | tf_op jit(solution)/shard_map/ppermute | solution.py:28
  106.1 3.6 %collective-permute-start.26 = (bf16[64,2048]{1,0:T(8,128)(2,1)S(1)}, bf16[64,2048]{1,0:T(8,128)(2,1)S(1)}, u32[]{:S(2)}, u32[]{:S(2)}) collective-permute-start(bf16[64,2048]{1,0:T(8,128)(2,1)S(1)} %get-tuple-element.72), channel_id=1, source_target_pairs={{0,96},{1,97},{2,98},{3,99},{4,100},{5,101},{6,102},{7,103},{8,120... | collective-permute-start | bytes 786440 | tf_op jit(solution)/shard_map/ppermute | solution.py:28
  109.7 2.2 %collective-permute-done.24 = bf16[64,2048]{1,0:T(8,128)(2,1)S(1)} collective-permute-done((bf16[64,2048]{1,0:T(8,128)(2,1)S(1)}, bf16[64,2048]{1,0:T(8,128)(2,1)S(1)}, u32[]{:S(2)}, u32[]{:S(2)}) %collective-permute-start.24) | collective-permute-done | bytes 262176 | tf_op jit(solution)/shard_map/ppermute | solution.py:28
  111.8 2.8 %collective-permute-done.25 = bf16[64,2048]{1,0:T(8,128)(2,1)S(1)} collective-permute-done((bf16[64,2048]{1,0:T(8,128)(2,1)S(1)}, bf16[64,2048]{1,0:T(8,128)(2,1)S(1)}, u32[]{:S(2)}, u32[]{:S(2)}) %collective-permute-start.25) | collective-permute-done | bytes 262176 | tf_op jit(solution)/shard_map/ppermute | solution.py:28
  (69 shorter events, 28.6 us)
Async XLA Ops:
  3.2 20.8 %all-to-all-start = ((bf16[16,4,4096]{2,1,0:T(4,128)(2,1)}), bf16[16,4,4096]{2,1,0:T(4,128)(2,1)S(1)}, u32[]{:S(2)}, u32[]{:S(2)}) async-start(bf16[16,4,4096]{2,1,0:T(4,128)(2,1)} %copy.12), calls=%async_computation | async-start | bytes 1048576 | tf_op jit(solution)/shard_map/all_to_all | solution.py:158
  24.1 17.4 %collective-permute-start.4 = (bf16[64,4096]{1,0:T(8,128)(2,1)S(1)}, bf16[64,4096]{1,0:T(8,128)(2,1)S(1)}, u32[]{:S(2)}, u32[]{:S(2)}) collective-permute-start(bf16[64,4096]{1,0:T(8,128)(2,1)S(1)} %reshape.445), channel_id=1, source_target_pairs={{0,4},{1,5},{2,6},{3,7},{4,0},{5,1},{6,2},{7,3},{8,12},{9,13},{10,... | collective-permute-start | bytes 1572872 | tf_op jit(solution)/shard_map/ppermute | solution.py:28
  27.2 9.5 %collective-permute-start.1 = (bf16[32,4096]{1,0:T(8,128)(2,1)S(1)}, bf16[32,4096]{1,0:T(8,128)(2,1)S(1)}, u32[]{:S(2)}, u32[]{:S(2)}) collective-permute-start(bf16[32,4096]{1,0:T(8,128)(2,1)S(1)} %get-tuple-element.75.refs_1_), channel_id=1, source_target_pairs={{0,3},{1,0},{2,1},{3,2},{4,7},{5,4},{6,5},{7,6},{8,9},{9,10},{10,1... | collective-permute-start | bytes 786440 | tf_op jit(solution)/shard_map/ppermute | solution.py:28
  27.2 12.2 %collective-permute-start.5 = (bf16[32,4096]{1,0:T(8,128)(2,1)S(1)}, bf16[32,4096]{1,0:T(8,128)(2,1)S(1)}, u32[]{:S(2)}, u32[]{:S(2)}) collective-permute-start(bf16[32,4096]{1,0:T(8,128)(2,1)S(1)} %get-tuple-element.75.refs_1_), channel_id=1, source_target_pairs={{0,1},{1,2},{2,3},{3,0},{4,5},{5,6},{6,7},{7,4},{8,11},{9,8},{10,9... | collective-permute-start | bytes 786440 | tf_op jit(solution)/shard_map/ppermute | solution.py:28
  29.9 11.6 %collective-permute-start.6 = (bf16[32,4096]{1,0:T(8,128)(2,1)S(1)}, bf16[32,4096]{1,0:T(8,128)(2,1)S(1)}, u32[]{:S(2)}, u32[]{:S(2)}) collective-permute-start(bf16[32,4096]{1,0:T(8,128)(2,1)S(1)} %get-tuple-element.76.refs_0_), channel_id=1, source_target_pairs={{0,3},{1,0},{2,1},{3,2},{4,7},{5,4},{6,5},{7,6},{8,9},{9,10},{10,1... | collective-permute-start | bytes 786440 | tf_op jit(solution)/shard_map/ppermute | solution.py:28
  36.7 8.2 %collective-permute-start.3 = (bf16[32,4096]{1,0:T(8,128)(2,1)S(1)}, bf16[32,4096]{1,0:T(8,128)(2,1)S(1)}, u32[]{:S(2)}, u32[]{:S(2)}) collective-permute-start(bf16[32,4096]{1,0:T(8,128)(2,1)S(1)} %collective-permute-done.1.refs_5_), channel_id=1, source_target_pairs={{0,3},{1,0},{2,1},{3,2},{4,7},{5,4},{6,5},{7,6},{8,9},{9,10},{10,1... | collective-permute-start | bytes 786440 | tf_op jit(solution)/shard_map/ppermute | solution.py:28
  36.7 9.3 %collective-permute-start.2 = (bf16[32,4096]{1,0:T(8,128)(2,1)S(1)}, bf16[32,4096]{1,0:T(8,128)(2,1)S(1)}, u32[]{:S(2)}, u32[]{:S(2)}) collective-permute-start(bf16[32,4096]{1,0:T(8,128)(2,1)S(1)} %collective-permute-done.refs_2_), channel_id=1, source_target_pairs={{0,1},{1,2},{2,3},{3,0},{4,5},{5,6},{6,7},{7,4},{8,11},{9,8},{10,9... | collective-permute-start | bytes 786440 | tf_op jit(solution)/shard_map/ppermute | solution.py:28
  41.5 15.2 %collective-permute-start.7 = (bf16[64,4096]{1,0:T(8,128)(2,1)S(1)}, bf16[64,4096]{1,0:T(8,128)(2,1)S(1)}, u32[]{:S(2)}, u32[]{:S(2)}) collective-permute-start(bf16[64,4096]{1,0:T(8,128)(2,1)S(1)} %collective-permute-done.4.refs_6_), channel_id=1, source_target_pairs={{0,1},{1,2},{2,3},{3,0},{4,5},{5,6},{6,7},{7,4},{8,11},{9,8},{10,9... | collective-permute-start | bytes 1572872 | tf_op jit(solution)/shard_map/ppermute | solution.py:28
  41.5 15.2 %collective-permute-start.8 = (bf16[64,4096]{1,0:T(8,128)(2,1)S(1)}, bf16[64,4096]{1,0:T(8,128)(2,1)S(1)}, u32[]{:S(2)}, u32[]{:S(2)}) collective-permute-start(bf16[64,4096]{1,0:T(8,128)(2,1)S(1)} %collective-permute-done.4.refs_6_), channel_id=1, source_target_pairs={{0,3},{1,0},{2,1},{3,2},{4,7},{5,4},{6,5},{7,6},{8,9},{9,10},{10,1... | collective-permute-start | bytes 1572872 | tf_op jit(solution)/shard_map/ppermute | solution.py:28
  44.9 8.1 %collective-permute-start.10 = (bf16[32,4096]{1,0:T(8,128)(2,1)S(1)}, bf16[32,4096]{1,0:T(8,128)(2,1)S(1)}, u32[]{:S(2)}, u32[]{:S(2)}) collective-permute-start(bf16[32,4096]{1,0:T(8,128)(2,1)S(1)} %collective-permute-done.3.refs_1_), channel_id=1, source_target_pairs={{0,4},{1,5},{2,6},{3,7},{4,0},{5,1},{6,2},{7,3},{8,12},{9,13},{10,... | collective-permute-start | bytes 786440 | tf_op jit(solution)/shard_map/ppermute | solution.py:28
  45.9 10.7 %collective-permute-start.9 = (bf16[32,4096]{1,0:T(8,128)(2,1)S(1)}, bf16[32,4096]{1,0:T(8,128)(2,1)S(1)}, u32[]{:S(2)}, u32[]{:S(2)}) collective-permute-start(bf16[32,4096]{1,0:T(8,128)(2,1)S(1)} %collective-permute-done.2.refs_0_), channel_id=1, source_target_pairs={{0,4},{1,5},{2,6},{3,7},{4,0},{5,1},{6,2},{7,3},{8,12},{9,13},{10,... | collective-permute-start | bytes 786440 | tf_op jit(solution)/shard_map/ppermute | solution.py:28
  58.2 18.7 %collective-permute-start.11 = (bf16[512,512]{1,0:T(8,128)(2,1)S(1)}, bf16[512,512]{1,0:T(8,128)(2,1)S(1)}, u32[]{:S(2)}, u32[]{:S(2)}) collective-permute-start(bf16[512,512]{1,0:T(8,128)(2,1)S(1)} %get-tuple-element.52), channel_id=1, source_target_pairs={{0,4},{1,5},{2,6},{3,7},{4,0},{5,1},{6,2},{7,3},{8,12},{9,13},{10,... | collective-permute-start | bytes 1572872 | tf_op jit(solution)/shard_map/ppermute | solution.py:28
  59.4 9.9 %collective-permute-start.16 = (bf16[256,512]{1,0:T(8,128)(2,1)S(1)}, bf16[256,512]{1,0:T(8,128)(2,1)S(1)}, u32[]{:S(2)}, u32[]{:S(2)}) collective-permute-start(bf16[256,512]{1,0:T(8,128)(2,1)S(1)} %get-tuple-element.54.refs_0_), channel_id=1, source_target_pairs={{0,1},{1,2},{2,3},{3,0},{4,5},{5,6},{6,7},{7,4},{8,11},{9,8},{10,9... | collective-permute-start | bytes 786440 | tf_op jit(solution)/shard_map/ppermute | solution.py:28
  62.2 9.1 %collective-permute-start.17 = (bf16[256,512]{1,0:T(8,128)(2,1)S(1)}, bf16[256,512]{1,0:T(8,128)(2,1)S(1)}, u32[]{:S(2)}, u32[]{:S(2)}) collective-permute-start(bf16[256,512]{1,0:T(8,128)(2,1)S(1)} %get-tuple-element.53.refs_1_), channel_id=1, source_target_pairs={{0,3},{1,0},{2,1},{3,2},{4,7},{5,4},{6,5},{7,6},{8,9},{9,10},{10,1... | collective-permute-start | bytes 786440 | tf_op jit(solution)/shard_map/ppermute | solution.py:28
  62.2 10.6 %collective-permute-start.12 = (bf16[256,512]{1,0:T(8,128)(2,1)S(1)}, bf16[256,512]{1,0:T(8,128)(2,1)S(1)}, u32[]{:S(2)}, u32[]{:S(2)}) collective-permute-start(bf16[256,512]{1,0:T(8,128)(2,1)S(1)} %get-tuple-element.53.refs_1_), channel_id=1, source_target_pairs={{0,1},{1,2},{2,3},{3,0},{4,5},{5,6},{6,7},{7,4},{8,11},{9,8},{10,9... | collective-permute-start | bytes 786440 | tf_op jit(solution)/shard_map/ppermute | solution.py:28
  64.9 12.1 %collective-permute-start.13 = (bf16[256,512]{1,0:T(8,128)(2,1)S(1)}, bf16[256,512]{1,0:T(8,128)(2,1)S(1)}, u32[]{:S(2)}, u32[]{:S(2)}) collective-permute-start(bf16[256,512]{1,0:T(8,128)(2,1)S(1)} %get-tuple-element.54.refs_0_), channel_id=1, source_target_pairs={{0,3},{1,0},{2,1},{3,2},{4,7},{5,4},{6,5},{7,6},{8,9},{9,10},{10,1... | collective-permute-start | bytes 786440 | tf_op jit(solution)/shard_map/ppermute | solution.py:28
  72.1 10.5 %collective-permute-start.20 = (bf16[256,512]{1,0:T(8,128)(2,1)S(1)}, bf16[256,512]{1,0:T(8,128)(2,1)S(1)}, u32[]{:S(2)}, u32[]{:S(2)}) collective-permute-start(bf16[256,512]{1,0:T(8,128)(2,1)S(1)} %collective-permute-done.17.refs_3_), channel_id=1, source_target_pairs={{0,3},{1,0},{2,1},{3,2},{4,7},{5,4},{6,5},{7,6},{8,9},{9,10},{10,1... | collective-permute-start | bytes 786440 | tf_op jit(solution)/shard_map/ppermute | solution.py:28
  76.9 12.2 %collective-permute-start.14 = (bf16[512,512]{1,0:T(8,128)(2,1)S(1)}, bf16[512,512]{1,0:T(8,128)(2,1)S(1)}, u32[]{:S(2)}, u32[]{:S(2)}) collective-permute-start(bf16[512,512]{1,0:T(8,128)(2,1)S(1)} %collective-permute-done.11.refs_4_), channel_id=1, source_target_pairs={{0,1},{1,2},{2,3},{3,0},{4,5},{5,6},{6,7},{7,4},{8,11},{9,8},{10,9... | collective-permute-start | bytes 1572872 | tf_op jit(solution)/shard_map/ppermute | solution.py:28
  76.9 16.8 %collective-permute-start.15 = (bf16[512,512]{1,0:T(8,128)(2,1)S(1)}, bf16[512,512]{1,0:T(8,128)(2,1)S(1)}, u32[]{:S(2)}, u32[]{:S(2)}) collective-permute-start(bf16[512,512]{1,0:T(8,128)(2,1)S(1)} %collective-permute-done.11.refs_4_), channel_id=1, source_target_pairs={{0,3},{1,0},{2,1},{3,2},{4,7},{5,4},{6,5},{7,6},{8,9},{9,10},{10,1... | collective-permute-start | bytes 1572872 | tf_op jit(solution)/shard_map/ppermute | solution.py:28
  78.4 9.2 %collective-permute-start.19 = (bf16[256,512]{1,0:T(8,128)(2,1)S(1)}, bf16[256,512]{1,0:T(8,128)(2,1)S(1)}, u32[]{:S(2)}, u32[]{:S(2)}) collective-permute-start(bf16[256,512]{1,0:T(8,128)(2,1)S(1)} %collective-permute-done.18.refs_5_), channel_id=1, source_target_pairs={{0,4},{1,5},{2,6},{3,7},{4,0},{5,1},{6,2},{7,3},{8,12},{9,13},{10,... | collective-permute-start | bytes 786440 | tf_op jit(solution)/shard_map/ppermute | solution.py:28
  99.4 10.3 %collective-permute-start.23 = (bf16[64,2048]{1,0:T(8,128)(2,1)S(1)}, bf16[64,2048]{1,0:T(8,128)(2,1)S(1)}, u32[]{:S(2)}, u32[]{:S(2)}) collective-permute-start(bf16[64,2048]{1,0:T(8,128)(2,1)S(1)} %get-tuple-element.71), channel_id=1, source_target_pairs={{8,24},{9,25},{10,26},{11,27},{12,28},{13,29},{14,30},{15,31},{24,... | collective-permute-start | bytes 786440 | tf_op jit(solution)/shard_map/ppermute | solution.py:28
  102.4 9.4 %collective-permute-start.24 = (bf16[64,2048]{1,0:T(8,128)(2,1)S(1)}, bf16[64,2048]{1,0:T(8,128)(2,1)S(1)}, u32[]{:S(2)}, u32[]{:S(2)}) collective-permute-start(bf16[64,2048]{1,0:T(8,128)(2,1)S(1)} %get-tuple-element.74), channel_id=1, source_target_pairs={{0,32},{1,33},{2,34},{3,35},{4,36},{5,37},{6,38},{7,39},{8,56},{9,... | collective-permute-start | bytes 786440 | tf_op jit(solution)/shard_map/ppermute | solution.py:28
  103.7 11.0 %collective-permute-start.25 = (bf16[64,2048]{1,0:T(8,128)(2,1)S(1)}, bf16[64,2048]{1,0:T(8,128)(2,1)S(1)}, u32[]{:S(2)}, u32[]{:S(2)}) collective-permute-start(bf16[64,2048]{1,0:T(8,128)(2,1)S(1)} %get-tuple-element.73), channel_id=1, source_target_pairs={{0,64},{1,65},{2,66},{3,67},{4,68},{5,69},{6,70},{7,71},{8,88},{9,... | collective-permute-start | bytes 786440 | tf_op jit(solution)/shard_map/ppermute | solution.py:28
  106.1 10.4 %collective-permute-start.26 = (bf16[64,2048]{1,0:T(8,128)(2,1)S(1)}, bf16[64,2048]{1,0:T(8,128)(2,1)S(1)}, u32[]{:S(2)}, u32[]{:S(2)}) collective-permute-start(bf16[64,2048]{1,0:T(8,128)(2,1)S(1)} %get-tuple-element.72), channel_id=1, source_target_pairs={{0,96},{1,97},{2,98},{3,99},{4,100},{5,101},{6,102},{7,103},{8,120... | collective-permute-start | bytes 786440 | tf_op jit(solution)/shard_map/ppermute | solution.py:28
  (8 other events, 52.4 us)

commit v5 on v3

--- a/solution.py
+++ b/solution.py
@@ -175,10 +175,8 @@
     slots = [here + x, here + left, here + right, there + x, here + over, there + left, there + right, there + over]
     own, place, slots = lax.optimization_barrier((own, place, jnp.stack(slots).astype(jnp.int32)))
 
-    near, far, _ = spread(own[:32], own[32:], own)
+    near, far, now = spread(own[:32], own[32:], own, columns_of(slots, 0, 5, sketch, 28)[0])
     first = precondition(near, h)
-    (now,) = columns_of(slots, 0, 5, sketch, 28)
-    far, first, now = lax.optimization_barrier((far, first, now))
     top, low, whole = precondition_order(far, h, first, place)
 
     near, far, (base, later) = spread(top, low, whole, columns_of(slots, 5, 3, sketch, 28, top, low, now))

time: 117 us -> 117 us (level)
    ppermute x28, waiting for transfers between devices: 28.1 us -> 29.3 us  [move(): return lax.ppermute(a, AXES, pairs(**offset))]
  transfers between devices with their start and end apart: 29 -> 29, of which waited for: 16 -> 15; matrix products, arithmetic and copies ran while one was open for 1% -> 1% of each run, Pallas kernels for 15% -> 15%
where the time goes in v5:
time: 117 us; the launch traced here: 116 us
  starting transfers between devices  50.2 us (43%)
  waiting for transfers between devices  39.4 us (34%)
  Pallas kernels  20.6 us (18%)
  local copies, waits for them, and re-layouts  3.52 us (3%)
  other arithmetic  1.46 us (1%)
    ppermute x28, starting transfers between devices, move(): return lax.ppermute(a, AXES, pairs(**offset))  40.7 us
    ppermute x28, waiting for transfers between devices, move(): return lax.ppermute(a, AXES, pairs(**offset))  29.3 us
    pallas_call x5, Pallas kernels, on_chip(): pl.pallas_call(kernel, in_specs=specs, out_specs=jax.tree.map(lambda _: p...  11.2 us
    all_to_all x1, waiting for transfers between devices, local(): lax.all_to_all(slotted, 'mod', split_axis=0, concat_axis=0, tiled=True)  10.1 us
    all_to_all x1, starting transfers between devices, local(): lax.all_to_all(slotted, 'mod', split_axis=0, concat_axis=0, tiled=True)  9.46 us
    pallas_call x2, Pallas kernels, columns_of(): pl.pallas_call(kernel, in_specs=[smem, pl.BlockSpec(memory_space=pl.ANY)]...  9.42 us
  transfers between devices with their start and end apart: 29, of which 15 were waited for; matrix products, arithmetic and copies ran while one was open for 1% of the time, Pallas kernels for 15%

profile of v5, /device:TPU:1, one launch (start us, length us, event | category | flops | bytes accessed | tf_op | source)
XLA Modules:
  0.0 116.5 jit_solution(159067332853435470)
XLA Ops:
  3.2 9.5 %all-to-all-start = ((bf16[16,4,4096]{2,1,0:T(4,128)(2,1)}), bf16[16,4,4096]{2,1,0:T(4,128)(2,1)S(1)}, u32[]{:S(2)}, u32[]{:S(2)}) async-start(bf16[16,4,4096]{2,1,0:T(4,128)(2,1)} %copy.12), calls=%async_computation | async-start | bytes 1048576 | tf_op jit(solution)/shard_map/all_to_all | solution.py:158
  13.9 10.1 %all-to-all-done = bf16[16,4,4096]{2,1,0:T(4,128)(2,1)S(1)} async-done(((bf16[16,4,4096]{2,1,0:T(4,128)(2,1)}), bf16[16,4,4096]{2,1,0:T(4,128)(2,1)S(1)}, u32[]{:S(2)}, u32[]{:S(2)}) %all-to-all-start) | async-done | bytes 524320 | tf_op jit(solution)/shard_map/all_to_all | solution.py:158
  27.4 2.7 %collective-permute-start.6 = (bf16[32,4096]{1,0:T(8,128)(2,1)S(1)}, bf16[32,4096]{1,0:T(8,128)(2,1)S(1)}, u32[]{:S(2)}, u32[]{:S(2)}) collective-permute-start(bf16[32,4096]{1,0:T(8,128)(2,1)S(1)} %get-tuple-element.62.refs_0_), channel_id=1, source_target_pairs={{0,3},{1,0},{2,1},{3,2},{4,7},{5,4},{6,5},{7,6},{8,11},{9,8},{10,9... | collective-permute-start | bytes 786440 | tf_op jit(solution)/shard_map/ppermute | solution.py:28
  30.1 5.0 %shard_map.55.refs_2_.refs_7_ = bf16[5,2048,512]{2,1,0:T(8,128)(2,1)S(1)} custom-call(s32[8]{0:T(128)S(1)} %stack.47.slots, bf16[2048,4096]{1,0:T(8,128)(2,1)} %bitcast.45), custom_call_target="tpu_custom_call" | custom-call | flops 1 | bytes 1 | tf_op jit(solution)/shard_map/pallas_call | solution.py:111
  40.6 3.0 %collective-permute-done.3.refs_1_ = bf16[32,4096]{1,0:T(8,128)(2,1)S(1)} collective-permute-done((bf16[32,4096]{1,0:T(8,128)(2,1)S(1)}, bf16[32,4096]{1,0:T(8,128)(2,1)S(1)}, u32[]{:S(2)}, u32[]{:S(2)}) %collective-permute-start.3) | collective-permute-done | bytes 262176 | tf_op jit(solution)/shard_map/ppermute | solution.py:28
  46.3 2.8 %collective-permute-done.10.refs_5_ = bf16[32,4096]{1,0:T(8,128)(2,1)S(1)} collective-permute-done((bf16[32,4096]{1,0:T(8,128)(2,1)S(1)}, bf16[32,4096]{1,0:T(8,128)(2,1)S(1)}, u32[]{:S(2)}, u32[]{:S(2)}) %collective-permute-start.10) | collective-permute-done | bytes 262176 | tf_op jit(solution)/shard_map/ppermute | solution.py:28
  49.1 3.6 %collective-permute-done.9.refs_4_ = bf16[32,4096]{1,0:T(8,128)(2,1)S(1)} collective-permute-done((bf16[32,4096]{1,0:T(8,128)(2,1)S(1)}, bf16[32,4096]{1,0:T(8,128)(2,1)S(1)}, u32[]{:S(2)}, u32[]{:S(2)}) %collective-permute-start.9) | collective-permute-done | bytes 262176 | tf_op jit(solution)/shard_map/ppermute | solution.py:28
  52.7 2.1 %collective-permute-done.8.refs_3_ = bf16[64,4096]{1,0:T(8,128)(2,1)S(1)} collective-permute-done((bf16[64,4096]{1,0:T(8,128)(2,1)S(1)}, bf16[64,4096]{1,0:T(8,128)(2,1)S(1)}, u32[]{:S(2)}, u32[]{:S(2)}) %collective-permute-start.8) | collective-permute-done | bytes 524320 | tf_op jit(solution)/shard_map/ppermute | solution.py:28
  60.2 2.7 %collective-permute-start.13 = (bf16[256,512]{1,0:T(8,128)(2,1)S(1)}, bf16[256,512]{1,0:T(8,128)(2,1)S(1)}, u32[]{:S(2)}, u32[]{:S(2)}) collective-permute-start(bf16[256,512]{1,0:T(8,128)(2,1)S(1)} %get-tuple-element.40.refs_0_), channel_id=1, source_target_pairs={{0,3},{1,0},{2,1},{3,2},{4,7},{5,4},{6,5},{7,6},{8,11},{9,8},{10,9... | collective-permute-start | bytes 786440 | tf_op jit(solution)/shard_map/ppermute | solution.py:28
  62.8 4.4 %shard_map.58 = (f32[512,2048]{1,0:T(8,128)S(1)}, bf16[3,2048,512]{2,1,0:T(8,128)(2,1)S(1)}) custom-call(s32[8]{0:T(128)S(1)} %stack.47.slots, bf16[2048,4096]{1,0:T(8,128)(2,1)} %bitcast.46, bf16[256,512]{1,0:T(8,128)(2,1)S(1)} %get-tuple-element.40.refs_0_, bf16[256,512]{1,0:T(8,128)(2,1)S(1)} %get-tuple-element.39.refs_1_, ...), custom_call_target="tpu_custom_call" | custom-call | flops 1 | bytes 1 | tf_op jit(solution)/shard_map/pallas_call | solution.py:111
  67.4 2.7 %collective-permute-start.20 = (bf16[256,512]{1,0:T(8,128)(2,1)S(1)}, bf16[256,512]{1,0:T(8,128)(2,1)S(1)}, u32[]{:S(2)}, u32[]{:S(2)}) collective-permute-start(bf16[256,512]{1,0:T(8,128)(2,1)S(1)} %collective-permute-done.17.refs_3_), channel_id=1, source_target_pairs={{0,3},{1,0},{2,1},{3,2},{4,7},{5,4},{6,5},{7,6},{8,11},{9,8},{10,9... | collective-permute-start | bytes 786440 | tf_op jit(solution)/shard_map/ppermute | solution.py:28
  70.2 2.7 %collective-permute-start.15 = (bf16[512,512]{1,0:T(8,128)(2,1)S(1)}, bf16[512,512]{1,0:T(8,128)(2,1)S(1)}, u32[]{:S(2)}, u32[]{:S(2)}) collective-permute-start(bf16[512,512]{1,0:T(8,128)(2,1)S(1)} %collective-permute-done.11.refs_4_), channel_id=1, source_target_pairs={{0,3},{1,0},{2,1},{3,2},{4,7},{5,4},{6,5},{7,6},{8,11},{9,8},{10,9... | collective-permute-start | bytes 1572872 | tf_op jit(solution)/shard_map/ppermute | solution.py:28
  72.8 2.3 %collective-permute-done.18.refs_5_ = bf16[256,512]{1,0:T(8,128)(2,1)S(1)} collective-permute-done((bf16[256,512]{1,0:T(8,128)(2,1)S(1)}, bf16[256,512]{1,0:T(8,128)(2,1)S(1)}, u32[]{:S(2)}, u32[]{:S(2)}) %collective-permute-start.18) | collective-permute-done | bytes 262176 | tf_op jit(solution)/shard_map/ppermute | solution.py:28
  76.6 4.6 %shard_map.59.refs_4_ = f32[512,2048]{1,0:T(8,128)S(1)} custom-call(bf16[256,512]{1,0:T(8,128)(2,1)S(1)} %collective-permute-done.16.refs_0_, bf16[256,512]{1,0:T(8,128)(2,1)S(1)} %collective-permute-done.12.refs_1_, bf16[256,512]{1,0:T(8,128)(2,1)S(1)} %collective-permute-done.13.refs_2_, bf16[256,512]{1,0:T(8,128)(2,1)S(1)} %collective-permute-done.17.refs_3_, ...), custom_call_target="tpu_custom_call" | custom-call | flops 1 | bytes 1 | tf_op jit(solution)/shard_map/pallas_call | solution.py:50
  81.2 2.2 %collective-permute-done.21.refs_2_ = bf16[256,512]{1,0:T(8,128)(2,1)S(1)} collective-permute-done((bf16[256,512]{1,0:T(8,128)(2,1)S(1)}, bf16[256,512]{1,0:T(8,128)(2,1)S(1)}, u32[]{:S(2)}, u32[]{:S(2)}) %collective-permute-start.21) | collective-permute-done | bytes 262176 | tf_op jit(solution)/shard_map/ppermute | solution.py:28
  83.5 2.3 %collective-permute-done.14.refs_0_ = bf16[512,512]{1,0:T(8,128)(2,1)S(1)} collective-permute-done((bf16[512,512]{1,0:T(8,128)(2,1)S(1)}, bf16[512,512]{1,0:T(8,128)(2,1)S(1)}, u32[]{:S(2)}, u32[]{:S(2)}) %collective-permute-start.14) | collective-permute-done | bytes 524320 | tf_op jit(solution)/shard_map/ppermute | solution.py:28
  88.2 5.3 %collective-permute-start.22 = (bf16[256,2048]{1,0:T(8,128)(2,1)S(1)}, bf16[256,2048]{1,0:T(8,128)(2,1)S(1)}, u32[]{:S(2)}, u32[]{:S(2)}) collective-permute-start(bf16[256,2048]{1,0:T(8,128)(2,1)S(1)} %shard_map.61), channel_id=1, source_target_pairs={{0,8},{1,9},{2,10},{3,11},{4,12},{5,13},{6,14},{7,15},{8,0},{9,1},... | collective-permute-start | bytes 3145736 | tf_op jit(solution)/shard_map/ppermute | solution.py:28
  93.5 1.9 %shard_map.60 = f32[256,2048]{1,0:T(8,128)S(1)} custom-call(bf16[512,512]{1,0:T(8,128)(2,1)S(1)} %collective-permute-done.14.refs_0_, bf16[512,512]{1,0:T(8,128)(2,1)S(1)} %collective-permute-done.15.refs_1_, bf16[256,512]{1,0:T(8,128)(2,1)S(1)} %collective-permute-done.21.refs_2_, bf16[3,2048,512]{2,1,0:T(8,128)(2,1)S(1)} %get-tuple-element.50.refs_3_, ...), custom_call_target="tpu_custom_call" | custom-call | flops 1 | bytes 1 | tf_op jit(solution)/shard_map/pallas_call | solution.py:50
  96.3 3.7 %collective-permute-start.23 = (bf16[64,2048]{1,0:T(8,128)(2,1)S(1)}, bf16[64,2048]{1,0:T(8,128)(2,1)S(1)}, u32[]{:S(2)}, u32[]{:S(2)}) collective-permute-start(bf16[64,2048]{1,0:T(8,128)(2,1)S(1)} %get-tuple-element.57), channel_id=1, source_target_pairs={{8,24},{9,25},{10,26},{11,27},{12,28},{13,29},{14,30},{15,31},{24,... | collective-permute-start | bytes 786440 | tf_op jit(solution)/shard_map/ppermute | solution.py:28
  101.2 2.7 %collective-permute-start.25 = (bf16[64,2048]{1,0:T(8,128)(2,1)S(1)}, bf16[64,2048]{1,0:T(8,128)(2,1)S(1)}, u32[]{:S(2)}, u32[]{:S(2)}) collective-permute-start(bf16[64,2048]{1,0:T(8,128)(2,1)S(1)} %get-tuple-element.59), channel_id=1, source_target_pairs={{0,64},{1,65},{2,66},{3,67},{4,68},{5,69},{6,70},{7,71},{8,88},{9,... | collective-permute-start | bytes 786440 | tf_op jit(solution)/shard_map/ppermute | solution.py:28
  104.0 2.7 %collective-permute-start.26 = (bf16[64,2048]{1,0:T(8,128)(2,1)S(1)}, bf16[64,2048]{1,0:T(8,128)(2,1)S(1)}, u32[]{:S(2)}, u32[]{:S(2)}) collective-permute-start(bf16[64,2048]{1,0:T(8,128)(2,1)S(1)} %get-tuple-element.58), channel_id=1, source_target_pairs={{0,96},{1,97},{2,98},{3,99},{4,100},{5,101},{6,102},{7,103},{8,120... | collective-permute-start | bytes 786440 | tf_op jit(solution)/shard_map/ppermute | solution.py:28
  106.6 2.6 %collective-permute-done.24 = bf16[64,2048]{1,0:T(8,128)(2,1)S(1)} collective-permute-done((bf16[64,2048]{1,0:T(8,128)(2,1)S(1)}, bf16[64,2048]{1,0:T(8,128)(2,1)S(1)}, u32[]{:S(2)}, u32[]{:S(2)}) %collective-permute-start.24) | collective-permute-done | bytes 262176 | tf_op jit(solution)/shard_map/ppermute | solution.py:28
  109.2 2.6 %collective-permute-done.25 = bf16[64,2048]{1,0:T(8,128)(2,1)S(1)} collective-permute-done((bf16[64,2048]{1,0:T(8,128)(2,1)S(1)}, bf16[64,2048]{1,0:T(8,128)(2,1)S(1)}, u32[]{:S(2)}, u32[]{:S(2)}) %collective-permute-start.25) | collective-permute-done | bytes 262176 | tf_op jit(solution)/shard_map/ppermute | solution.py:28
  111.8 2.1 %collective-permute-done.26 = bf16[64,2048]{1,0:T(8,128)(2,1)S(1)} collective-permute-done((bf16[64,2048]{1,0:T(8,128)(2,1)S(1)}, bf16[64,2048]{1,0:T(8,128)(2,1)S(1)}, u32[]{:S(2)}, u32[]{:S(2)}) %collective-permute-start.26) | collective-permute-done | bytes 262176 | tf_op jit(solution)/shard_map/ppermute | solution.py:28
  (69 shorter events, 30.1 us)
Async XLA Ops:
  3.2 20.8 %all-to-all-start = ((bf16[16,4,4096]{2,1,0:T(4,128)(2,1)}), bf16[16,4,4096]{2,1,0:T(4,128)(2,1)S(1)}, u32[]{:S(2)}, u32[]{:S(2)}) async-start(bf16[16,4,4096]{2,1,0:T(4,128)(2,1)} %copy.12), calls=%async_computation | async-start | bytes 1048576 | tf_op jit(solution)/shard_map/all_to_all | solution.py:158
  24.1 13.8 %collective-permute-start.4 = (bf16[64,4096]{1,0:T(8,128)(2,1)S(1)}, bf16[64,4096]{1,0:T(8,128)(2,1)S(1)}, u32[]{:S(2)}, u32[]{:S(2)}) collective-permute-start(bf16[64,4096]{1,0:T(8,128)(2,1)S(1)} %reshape.441), channel_id=1, source_target_pairs={{0,4},{1,5},{2,6},{3,7},{4,0},{5,1},{6,2},{7,3},{8,12},{9,13},{10,... | collective-permute-start | bytes 1572872 | tf_op jit(solution)/shard_map/ppermute | solution.py:28
  24.7 10.4 %collective-permute-start = (bf16[32,4096]{1,0:T(8,128)(2,1)S(1)}, bf16[32,4096]{1,0:T(8,128)(2,1)S(1)}, u32[]{:S(2)}, u32[]{:S(2)}) collective-permute-start(bf16[32,4096]{1,0:T(8,128)(2,1)S(1)} %get-tuple-element.62.refs_0_), channel_id=1, source_target_pairs={{0,1},{1,2},{2,3},{3,0},{4,5},{5,6},{6,7},{7,4},{8,9},{9,10},{10,1... | collective-permute-start | bytes 786440 | tf_op jit(solution)/shard_map/ppermute | solution.py:28
  25.9 9.1 %collective-permute-start.1 = (bf16[32,4096]{1,0:T(8,128)(2,1)S(1)}, bf16[32,4096]{1,0:T(8,128)(2,1)S(1)}, u32[]{:S(2)}, u32[]{:S(2)}) collective-permute-start(bf16[32,4096]{1,0:T(8,128)(2,1)S(1)} %get-tuple-element.61.refs_1_), channel_id=1, source_target_pairs={{0,3},{1,0},{2,1},{3,2},{4,7},{5,4},{6,5},{7,6},{8,11},{9,8},{10,9... | collective-permute-start | bytes 786440 | tf_op jit(solution)/shard_map/ppermute | solution.py:28
  27.4 10.5 %collective-permute-start.5 = (bf16[32,4096]{1,0:T(8,128)(2,1)S(1)}, bf16[32,4096]{1,0:T(8,128)(2,1)S(1)}, u32[]{:S(2)}, u32[]{:S(2)}) collective-permute-start(bf16[32,4096]{1,0:T(8,128)(2,1)S(1)} %get-tuple-element.61.refs_1_), channel_id=1, source_target_pairs={{0,1},{1,2},{2,3},{3,0},{4,5},{5,6},{6,7},{7,4},{8,9},{9,10},{10,1... | collective-permute-start | bytes 786440 | tf_op jit(solution)/shard_map/ppermute | solution.py:28
  27.4 10.5 %collective-permute-start.6 = (bf16[32,4096]{1,0:T(8,128)(2,1)S(1)}, bf16[32,4096]{1,0:T(8,128)(2,1)S(1)}, u32[]{:S(2)}, u32[]{:S(2)}) collective-permute-start(bf16[32,4096]{1,0:T(8,128)(2,1)S(1)} %get-tuple-element.62.refs_0_), channel_id=1, source_target_pairs={{0,3},{1,0},{2,1},{3,2},{4,7},{5,4},{6,5},{7,6},{8,11},{9,8},{10,9... | collective-permute-start | bytes 786440 | tf_op jit(solution)/shard_map/ppermute | solution.py:28
  35.1 8.5 %collective-permute-start.3 = (bf16[32,4096]{1,0:T(8,128)(2,1)S(1)}, bf16[32,4096]{1,0:T(8,128)(2,1)S(1)}, u32[]{:S(2)}, u32[]{:S(2)}) collective-permute-start(bf16[32,4096]{1,0:T(8,128)(2,1)S(1)} %collective-permute-done.1.refs_5_), channel_id=1, source_target_pairs={{0,3},{1,0},{2,1},{3,2},{4,7},{5,4},{6,5},{7,6},{8,11},{9,8},{10,9... | collective-permute-start | bytes 786440 | tf_op jit(solution)/shard_map/ppermute | solution.py:28
  35.2 9.4 %collective-permute-start.2 = (bf16[32,4096]{1,0:T(8,128)(2,1)S(1)}, bf16[32,4096]{1,0:T(8,128)(2,1)S(1)}, u32[]{:S(2)}, u32[]{:S(2)}) collective-permute-start(bf16[32,4096]{1,0:T(8,128)(2,1)S(1)} %collective-permute-done.refs_2_), channel_id=1, source_target_pairs={{0,1},{1,2},{2,3},{3,0},{4,5},{5,6},{6,7},{7,4},{8,9},{9,10},{10,1... | collective-permute-start | bytes 786440 | tf_op jit(solution)/shard_map/ppermute | solution.py:28
  37.9 14.8 %collective-permute-start.7 = (bf16[64,4096]{1,0:T(8,128)(2,1)S(1)}, bf16[64,4096]{1,0:T(8,128)(2,1)S(1)}, u32[]{:S(2)}, u32[]{:S(2)}) collective-permute-start(bf16[64,4096]{1,0:T(8,128)(2,1)S(1)} %collective-permute-done.4.refs_6_), channel_id=1, source_target_pairs={{0,1},{1,2},{2,3},{3,0},{4,5},{5,6},{6,7},{7,4},{8,9},{9,10},{10,1... | collective-permute-start | bytes 1572872 | tf_op jit(solution)/shard_map/ppermute | solution.py:28
  38.8 15.9 %collective-permute-start.8 = (bf16[64,4096]{1,0:T(8,128)(2,1)S(1)}, bf16[64,4096]{1,0:T(8,128)(2,1)S(1)}, u32[]{:S(2)}, u32[]{:S(2)}) collective-permute-start(bf16[64,4096]{1,0:T(8,128)(2,1)S(1)} %collective-permute-done.4.refs_6_), channel_id=1, source_target_pairs={{0,3},{1,0},{2,1},{3,2},{4,7},{5,4},{6,5},{7,6},{8,11},{9,8},{10,9... | collective-permute-start | bytes 1572872 | tf_op jit(solution)/shard_map/ppermute | solution.py:28
  44.6 8.1 %collective-permute-start.9 = (bf16[32,4096]{1,0:T(8,128)(2,1)S(1)}, bf16[32,4096]{1,0:T(8,128)(2,1)S(1)}, u32[]{:S(2)}, u32[]{:S(2)}) collective-permute-start(bf16[32,4096]{1,0:T(8,128)(2,1)S(1)} %collective-permute-done.2.refs_0_), channel_id=1, source_target_pairs={{0,4},{1,5},{2,6},{3,7},{4,0},{5,1},{6,2},{7,3},{8,12},{9,13},{10,... | collective-permute-start | bytes 786440 | tf_op jit(solution)/shard_map/ppermute | solution.py:28
  56.3 13.7 %collective-permute-start.11 = (bf16[512,512]{1,0:T(8,128)(2,1)S(1)}, bf16[512,512]{1,0:T(8,128)(2,1)S(1)}, u32[]{:S(2)}, u32[]{:S(2)}) collective-permute-start(bf16[512,512]{1,0:T(8,128)(2,1)S(1)} %get-tuple-element.38), channel_id=1, source_target_pairs={{0,4},{1,5},{2,6},{3,7},{4,0},{5,1},{6,2},{7,3},{8,12},{9,13},{10,... | collective-permute-start | bytes 1572872 | tf_op jit(solution)/shard_map/ppermute | solution.py:28
  57.5 9.8 %collective-permute-start.16 = (bf16[256,512]{1,0:T(8,128)(2,1)S(1)}, bf16[256,512]{1,0:T(8,128)(2,1)S(1)}, u32[]{:S(2)}, u32[]{:S(2)}) collective-permute-start(bf16[256,512]{1,0:T(8,128)(2,1)S(1)} %get-tuple-element.40.refs_0_), channel_id=1, source_target_pairs={{0,1},{1,2},{2,3},{3,0},{4,5},{5,6},{6,7},{7,4},{8,9},{9,10},{10,1... | collective-permute-start | bytes 786440 | tf_op jit(solution)/shard_map/ppermute | solution.py:28
  58.4 8.9 %collective-permute-start.17 = (bf16[256,512]{1,0:T(8,128)(2,1)S(1)}, bf16[256,512]{1,0:T(8,128)(2,1)S(1)}, u32[]{:S(2)}, u32[]{:S(2)}) collective-permute-start(bf16[256,512]{1,0:T(8,128)(2,1)S(1)} %get-tuple-element.39.refs_1_), channel_id=1, source_target_pairs={{0,3},{1,0},{2,1},{3,2},{4,7},{5,4},{6,5},{7,6},{8,11},{9,8},{10,9... | collective-permute-start | bytes 786440 | tf_op jit(solution)/shard_map/ppermute | solution.py:28
  60.2 9.9 %collective-permute-start.12 = (bf16[256,512]{1,0:T(8,128)(2,1)S(1)}, bf16[256,512]{1,0:T(8,128)(2,1)S(1)}, u32[]{:S(2)}, u32[]{:S(2)}) collective-permute-start(bf16[256,512]{1,0:T(8,128)(2,1)S(1)} %get-tuple-element.39.refs_1_), channel_id=1, source_target_pairs={{0,1},{1,2},{2,3},{3,0},{4,5},{5,6},{6,7},{7,4},{8,9},{9,10},{10,1... | collective-permute-start | bytes 786440 | tf_op jit(solution)/shard_map/ppermute | solution.py:28
  60.2 9.9 %collective-permute-start.13 = (bf16[256,512]{1,0:T(8,128)(2,1)S(1)}, bf16[256,512]{1,0:T(8,128)(2,1)S(1)}, u32[]{:S(2)}, u32[]{:S(2)}) collective-permute-start(bf16[256,512]{1,0:T(8,128)(2,1)S(1)} %get-tuple-element.40.refs_0_), channel_id=1, source_target_pairs={{0,3},{1,0},{2,1},{3,2},{4,7},{5,4},{6,5},{7,6},{8,11},{9,8},{10,9... | collective-permute-start | bytes 786440 | tf_op jit(solution)/shard_map/ppermute | solution.py:28
  67.4 8.2 %collective-permute-start.20 = (bf16[256,512]{1,0:T(8,128)(2,1)S(1)}, bf16[256,512]{1,0:T(8,128)(2,1)S(1)}, u32[]{:S(2)}, u32[]{:S(2)}) collective-permute-start(bf16[256,512]{1,0:T(8,128)(2,1)S(1)} %collective-permute-done.17.refs_3_), channel_id=1, source_target_pairs={{0,3},{1,0},{2,1},{3,2},{4,7},{5,4},{6,5},{7,6},{8,11},{9,8},{10,9... | collective-permute-start | bytes 786440 | tf_op jit(solution)/shard_map/ppermute | solution.py:28
  70.1 15.7 %collective-permute-start.14 = (bf16[512,512]{1,0:T(8,128)(2,1)S(1)}, bf16[512,512]{1,0:T(8,128)(2,1)S(1)}, u32[]{:S(2)}, u32[]{:S(2)}) collective-permute-start(bf16[512,512]{1,0:T(8,128)(2,1)S(1)} %collective-permute-done.11.refs_4_), channel_id=1, source_target_pairs={{0,1},{1,2},{2,3},{3,0},{4,5},{5,6},{6,7},{7,4},{8,9},{9,10},{10,1... | collective-permute-start | bytes 1572872 | tf_op jit(solution)/shard_map/ppermute | solution.py:28
  70.2 16.1 %collective-permute-start.15 = (bf16[512,512]{1,0:T(8,128)(2,1)S(1)}, bf16[512,512]{1,0:T(8,128)(2,1)S(1)}, u32[]{:S(2)}, u32[]{:S(2)}) collective-permute-start(bf16[512,512]{1,0:T(8,128)(2,1)S(1)} %collective-permute-done.11.refs_4_), channel_id=1, source_target_pairs={{0,3},{1,0},{2,1},{3,2},{4,7},{5,4},{6,5},{7,6},{8,11},{9,8},{10,9... | collective-permute-start | bytes 1572872 | tf_op jit(solution)/shard_map/ppermute | solution.py:28
  75.6 7.9 %collective-permute-start.21 = (bf16[256,512]{1,0:T(8,128)(2,1)S(1)}, bf16[256,512]{1,0:T(8,128)(2,1)S(1)}, u32[]{:S(2)}, u32[]{:S(2)}) collective-permute-start(bf16[256,512]{1,0:T(8,128)(2,1)S(1)} %collective-permute-done.20.refs_6_), channel_id=1, source_target_pairs={{0,4},{1,5},{2,6},{3,7},{4,0},{5,1},{6,2},{7,3},{8,12},{9,13},{10,... | collective-permute-start | bytes 786440 | tf_op jit(solution)/shard_map/ppermute | solution.py:28
  96.3 10.3 %collective-permute-start.23 = (bf16[64,2048]{1,0:T(8,128)(2,1)S(1)}, bf16[64,2048]{1,0:T(8,128)(2,1)S(1)}, u32[]{:S(2)}, u32[]{:S(2)}) collective-permute-start(bf16[64,2048]{1,0:T(8,128)(2,1)S(1)} %get-tuple-element.57), channel_id=1, source_target_pairs={{8,24},{9,25},{10,26},{11,27},{12,28},{13,29},{14,30},{15,31},{24,... | collective-permute-start | bytes 786440 | tf_op jit(solution)/shard_map/ppermute | solution.py:28
  100.0 9.2 %collective-permute-start.24 = (bf16[64,2048]{1,0:T(8,128)(2,1)S(1)}, bf16[64,2048]{1,0:T(8,128)(2,1)S(1)}, u32[]{:S(2)}, u32[]{:S(2)}) collective-permute-start(bf16[64,2048]{1,0:T(8,128)(2,1)S(1)} %get-tuple-element.60), channel_id=1, source_target_pairs={{0,32},{1,33},{2,34},{3,35},{4,36},{5,37},{6,38},{7,39},{8,56},{9,... | collective-permute-start | bytes 786440 | tf_op jit(solution)/shard_map/ppermute | solution.py:28
  101.2 10.5 %collective-permute-start.25 = (bf16[64,2048]{1,0:T(8,128)(2,1)S(1)}, bf16[64,2048]{1,0:T(8,128)(2,1)S(1)}, u32[]{:S(2)}, u32[]{:S(2)}) collective-permute-start(bf16[64,2048]{1,0:T(8,128)(2,1)S(1)} %get-tuple-element.59), channel_id=1, source_target_pairs={{0,64},{1,65},{2,66},{3,67},{4,68},{5,69},{6,70},{7,71},{8,88},{9,... | collective-permute-start | bytes 786440 | tf_op jit(solution)/shard_map/ppermute | solution.py:28
  104.0 9.9 %collective-permute-start.26 = (bf16[64,2048]{1,0:T(8,128)(2,1)S(1)}, bf16[64,2048]{1,0:T(8,128)(2,1)S(1)}, u32[]{:S(2)}, u32[]{:S(2)}) collective-permute-start(bf16[64,2048]{1,0:T(8,128)(2,1)S(1)} %get-tuple-element.58), channel_id=1, source_target_pairs={{0,96},{1,97},{2,98},{3,99},{4,100},{5,101},{6,102},{7,103},{8,120... | collective-permute-start | bytes 786440 | tf_op jit(solution)/shard_map/ppermute | solution.py:28
  (8 other events, 65.3 us)
